TPU v7x, 32 devices: a whole 2x2x4 slice. The times are simulated.
32 devices in a mesh: ctx: 8 (over z, y), fsdp: 4 (over x, core).
Axes of the slice: x: 2, y: 2, z: 4, core: 2. Of those that a mesh axis runs over, the one named last changes fastest.
Arguments:
- hidden_in: bfloat16 [8, 8, 256, 576], P('fsdp', 'ctx'), may hold values from -6 to 6
- cotangent: bfloat16 [8, 8, 256, 576], P('fsdp', 'ctx'), may hold values from -6 to 6
- span_table: int32 [8], replicated, may hold values from 0 to 7, as said below
- positions: int32 [8, 8, 256], P('fsdp', 'ctx'), may hold values from 0 to 4095, as said below
- attn_gain: bfloat16 [576], P('fsdp'), may hold values from 0.5 to 1.5
- w_query: bfloat16 [576, 576], P('fsdp'), may hold values from -0.25 to 0.25
- w_key: bfloat16 [576, 192], P('fsdp'), may hold values from -0.25 to 0.25
- w_value: bfloat16 [576, 192], P('fsdp'), may hold values from -0.25 to 0.25
- w_out: bfloat16 [576, 576], P('fsdp'), may hold values from -3 to 3
- ffn_gain: bfloat16 [576], P('fsdp'), may hold values from 0.5 to 1.5
- w_gate: bfloat16 [576, 1536], P('fsdp'), may hold values from -0.25 to 0.25
- w_up: bfloat16 [576, 1536], P('fsdp'), may hold values from -0.25 to 0.25
- w_down: bfloat16 [1536, 576], P('fsdp'), may hold values from -0.15625 to 0.15625
Outputs:
- hidden_out: bfloat16 [8, 8, 256, 576], P('fsdp', 'ctx')
- grad_input: float32 [8, 8, 256, 576], P('fsdp', 'ctx')
- grad_query: float32 [576, 576], P('fsdp')
- grad_key: float32 [576, 192], P('fsdp')
- grad_value: float32 [576, 192], P('fsdp')
- grad_out: float32 [576, 576], P('fsdp')
- grad_gate: float32 [576, 1536], P('fsdp')
- grad_up: float32 [576, 1536], P('fsdp')
- grad_down: float32 [1536, 576], P('fsdp')
- grad_attn_gain: float32 [576], P('fsdp')
- grad_ffn_gain: float32 [576], P('fsdp')
Inputs may be any that keep to these rules, and one draw needn't show every extreme that they name: `span_table`: a permutation of 0 to 7. `positions`: a token's position is its place in the sequence (by span_table) plus a start of its own sequence; the starts lie in 0 to 2048.
All inputs are finite; a program needn't handle non-finite values.
Results may differ from a plain program's by a relative error of at most 0.017.
Values may be sent and summed in bfloat16 or wider, within the bound.
A program may use at most 128 MiB of HBM per device.

v0:
```python
import math

import jax
import jax.numpy as jnp
from jax import lax
from jax.sharding import PartitionSpec as P

HQ = 9
HK = 3
HD = 64


EPS = 1e-05
THETA = 100000.0


def rotate(vector, cosine, sine):
    half_dim = vector.shape[-1] // 2
    first = vector[..., :half_dim]
    second = vector[..., half_dim:]
    return jnp.concatenate(
        [first * cosine - second * sine, second * cosine + first * sine], axis=-1
    )


def rope_tables(place, head_dim):
    half_dim = head_dim // 2
    inverse = jnp.exp(jnp.arange(half_dim, dtype=jnp.float32) * (-math.log(THETA) / half_dim))
    angles = place.astype(jnp.float32)[:, None] * inverse[None, :]
    return (jnp.cos(angles)[:, None, :], jnp.sin(angles)[:, None, :])


def norm_back(vector, inverse, gain_vec, incoming):
    scaled = incoming * gain_vec
    gain_grad = jnp.sum(incoming * vector * inverse, axis=0)
    vector_grad = inverse * scaled - vector * (inverse * inverse * inverse) * jnp.mean(
        scaled * vector, axis=-1, keepdims=True
    )
    return (vector_grad, gain_grad)


def shards(
    hidden_in,
    cotangent,
    span_table,
    positions,
    attn_gain,
    w_query,
    w_key,
    w_value,
    w_out,
    ffn_gain,
    w_gate,
    w_up,
    w_down,
):
    seq_count = hidden_in.shape[0]
    pair_rows = hidden_in.shape[2]
    width = hidden_in.shape[3]
    span_rows = pair_rows // 2
    ctx_count = lax.axis_size("ctx")
    full_len = ctx_count * pair_rows
    row_count = seq_count * pair_rows
    group_size = HQ // HK
    score_scale = 1.0 / math.sqrt(HD)
    f32 = jnp.float32
    bf16 = jnp.bfloat16
    columns = jnp.arange(pair_rows, dtype=jnp.int32)
    span_ids = jnp.where(
        columns[None, :] < span_rows, span_table[:, None], 2 * ctx_count - 1 - span_table[:, None]
    )
    key_order = (span_ids * span_rows + columns[None, :] % span_rows).reshape(full_len)
    own_order = lax.dynamic_slice_in_dim(key_order, lax.axis_index("ctx") * pair_rows, pair_rows)
    allowed = (key_order[None, :] <= own_order[:, None])[None, :, :]
    weights = (
        lax.all_gather(w_query, "fsdp", axis=0, tiled=True),
        lax.all_gather(w_key, "fsdp", axis=0, tiled=True),
        lax.all_gather(w_value, "fsdp", axis=0, tiled=True),
        lax.all_gather(w_out, "fsdp", axis=0, tiled=True),
        lax.all_gather(w_gate, "fsdp", axis=0, tiled=True),
        lax.all_gather(w_up, "fsdp", axis=0, tiled=True),
        lax.all_gather(w_down, "fsdp", axis=0, tiled=True),
        lax.all_gather(attn_gain, "fsdp", axis=0, tiled=True),
        lax.all_gather(ffn_gain, "fsdp", axis=0, tiled=True),
    )
    wq_all, wk_all, wv_all, wo_all, wg_all, wu_all, wd_all, gain_first, gain_second = weights
    cosine, sine = rope_tables(positions.reshape(row_count), HD)
    x_rows = hidden_in.reshape(row_count, width).astype(f32)
    inverse_one = lax.rsqrt(jnp.mean(x_rows * x_rows, axis=-1, keepdims=True) + EPS)
    first_in = (x_rows * inverse_one * gain_first.astype(f32)).astype(bf16)
    query_rows = rotate(
        jnp.dot(first_in, wq_all, preferred_element_type=f32).reshape(row_count, HQ, HD),
        cosine,
        sine,
    ).astype(bf16)
    key_rows = rotate(
        jnp.dot(first_in, wk_all, preferred_element_type=f32).reshape(row_count, HK, HD),
        cosine,
        sine,
    ).astype(bf16)
    value_rows = jnp.dot(first_in, wv_all, preferred_element_type=f32).astype(bf16)
    outgoing = (
        key_rows.reshape(seq_count, pair_rows, HK * HD),
        value_rows.reshape(seq_count, pair_rows, HK * HD),
    )
    all_keys, all_values = (
        lax.all_gather(outgoing[0], "ctx", axis=1, tiled=True),
        lax.all_gather(outgoing[1], "ctx", axis=1, tiled=True),
    )
    query_seqs = query_rows.reshape(seq_count, pair_rows, HK, group_size, HD)

    def forward_group(parts):
        query_grp, key_grp, value_grp = parts
        scores = (
            jnp.einsum("qrd,kd->rqk", query_grp, key_grp, preferred_element_type=f32) * score_scale
        )
        scores = jnp.where(allowed, scores, -1e30)
        row_max = jnp.max(scores, axis=-1, keepdims=True)
        raised = jnp.exp(scores - row_max)
        row_sum = jnp.sum(raised, axis=-1, keepdims=True)
        probs = (raised / row_sum).astype(bf16)
        attended = jnp.einsum("rqk,kd->qrd", probs, value_grp, preferred_element_type=f32)
        return (attended.astype(bf16), (row_max + jnp.log(row_sum))[..., 0])

    def forward_seq(inputs):
        query_blk, key_blk, value_blk = inputs
        key_full = jnp.moveaxis(key_blk.reshape(full_len, HK, HD), 1, 0)
        value_full = jnp.moveaxis(value_blk.reshape(full_len, HK, HD), 1, 0)
        attended, log_sum = lax.map(
            forward_group, (jnp.moveaxis(query_blk, 1, 0), key_full, value_full)
        )
        return (jnp.moveaxis(attended, 0, 1).reshape(pair_rows, HQ * HD), log_sum)

    mixed_seqs, log_sums = lax.map(forward_seq, (query_seqs, all_keys, all_values))
    mixed_rows = mixed_seqs.reshape(row_count, HQ * HD)
    middle = x_rows + jnp.dot(mixed_rows, wo_all, preferred_element_type=f32)
    inverse_two = lax.rsqrt(jnp.mean(middle * middle, axis=-1, keepdims=True) + EPS)
    second_in = (middle * inverse_two * gain_second.astype(f32)).astype(bf16)
    gate_proj = jnp.dot(second_in, wg_all, preferred_element_type=f32)
    up_proj = jnp.dot(second_in, wu_all, preferred_element_type=f32)
    hidden = (jax.nn.silu(gate_proj) * up_proj).astype(bf16)
    out_rows = middle + jnp.dot(hidden, wd_all, preferred_element_type=f32)
    result = out_rows.astype(bf16).reshape(hidden_in.shape)
    weights_back = (
        lax.all_gather(w_query, "fsdp", axis=0, tiled=True),
        lax.all_gather(w_key, "fsdp", axis=0, tiled=True),
        lax.all_gather(w_value, "fsdp", axis=0, tiled=True),
        lax.all_gather(w_out, "fsdp", axis=0, tiled=True),
        lax.all_gather(w_gate, "fsdp", axis=0, tiled=True),
        lax.all_gather(w_up, "fsdp", axis=0, tiled=True),
        lax.all_gather(w_down, "fsdp", axis=0, tiled=True),
        lax.all_gather(attn_gain, "fsdp", axis=0, tiled=True),
        lax.all_gather(ffn_gain, "fsdp", axis=0, tiled=True),
    )
    wq_back, wk_back, wv_back, wo_back, wg_back, wu_back, wd_back, gain_first_b, gain_second_b = (
        weights_back
    )
    grad_rows = cotangent.reshape(row_count, width).astype(f32)
    grad_branch = grad_rows.astype(bf16)
    dw_down = jnp.einsum("rf,rd->fd", hidden, grad_branch, preferred_element_type=f32)
    grad_hidden = jnp.einsum("rd,fd->rf", grad_branch, wd_back, preferred_element_type=f32)
    sigmoid_gate = jax.nn.sigmoid(gate_proj)
    grad_gate_proj = (
        grad_hidden * up_proj * sigmoid_gate * (1.0 + gate_proj * (1.0 - sigmoid_gate))
    ).astype(bf16)
    grad_up_proj = (grad_hidden * gate_proj * sigmoid_gate).astype(bf16)
    dw_gate = jnp.einsum("rd,rf->df", second_in, grad_gate_proj, preferred_element_type=f32)
    dw_up = jnp.einsum("rd,rf->df", second_in, grad_up_proj, preferred_element_type=f32)
    grad_second = jnp.einsum(
        "rf,df->rd", grad_gate_proj, wg_back, preferred_element_type=f32
    ) + jnp.einsum("rf,df->rd", grad_up_proj, wu_back, preferred_element_type=f32)
    grad_norm_two, dg_second = norm_back(
        middle, inverse_two, gain_second_b.astype(f32), grad_second
    )
    grad_middle = grad_rows + grad_norm_two
    grad_attn = grad_middle.astype(bf16)
    dw_out = jnp.einsum("rf,rd->fd", mixed_rows, grad_attn, preferred_element_type=f32)
    grad_mixed = jnp.einsum("rd,fd->rf", grad_attn, wo_back, preferred_element_type=f32).astype(
        bf16
    )
    grad_mixed_seqs = grad_mixed.reshape(seq_count, pair_rows, HK, group_size, HD)
    keys_back, values_back = (
        lax.all_gather(outgoing[0], "ctx", axis=1, tiled=True),
        lax.all_gather(outgoing[1], "ctx", axis=1, tiled=True),
    )

    def backward_group(parts):
        query_grp, key_grp, value_grp, grad_grp, log_grp = parts
        scores = (
            jnp.einsum("qrd,kd->rqk", query_grp, key_grp, preferred_element_type=f32) * score_scale
        )
        scores = jnp.where(allowed, scores, -1e30)
        probs = jnp.exp(scores - log_grp[..., None])
        grad_probs = jnp.einsum("qrd,kd->rqk", grad_grp, value_grp, preferred_element_type=f32)
        row_dot = jnp.sum(grad_probs * probs, axis=-1, keepdims=True)
        grad_scores = (probs * (grad_probs - row_dot)).astype(bf16)
        grad_query_grp = (
            jnp.einsum("rqk,kd->qrd", grad_scores, key_grp, preferred_element_type=f32)
            * score_scale
        )
        grad_key_grp = (
            jnp.einsum("rqk,qrd->kd", grad_scores, query_grp, preferred_element_type=f32)
            * score_scale
        )
        grad_value_grp = jnp.einsum(
            "rqk,qrd->kd", probs.astype(bf16), grad_grp, preferred_element_type=f32
        )
        return (grad_query_grp, grad_key_grp, grad_value_grp)

    def backward_seq(inputs):
        query_blk, key_blk, value_blk, grad_blk, log_blk = inputs
        key_full = jnp.moveaxis(key_blk.reshape(full_len, HK, HD), 1, 0)
        value_full = jnp.moveaxis(value_blk.reshape(full_len, HK, HD), 1, 0)
        grad_query_all, grad_key_all, grad_value_all = lax.map(
            backward_group,
            (
                jnp.moveaxis(query_blk, 1, 0),
                key_full,
                value_full,
                jnp.moveaxis(grad_blk, 1, 0),
                log_blk,
            ),
        )
        return (
            jnp.moveaxis(grad_query_all, 0, 1).reshape(pair_rows, HQ * HD),
            jnp.moveaxis(grad_key_all, 0, 1).reshape(full_len, HK * HD),
            jnp.moveaxis(grad_value_all, 0, 1).reshape(full_len, HK * HD),
        )

    grad_query_seqs, grad_key_seqs, grad_value_seqs = lax.map(
        backward_seq, (query_seqs, keys_back, values_back, grad_mixed_seqs, log_sums)
    )
    own_key_grad, own_value_grad = (
        lax.psum_scatter(grad_key_seqs, "ctx", scatter_dimension=1, tiled=True),
        lax.psum_scatter(grad_value_seqs, "ctx", scatter_dimension=1, tiled=True),
    )
    grad_query_lin = (
        rotate(grad_query_seqs.reshape(row_count, HQ, HD), cosine, -sine)
        .reshape(row_count, HQ * HD)
        .astype(bf16)
    )
    grad_key_lin = (
        rotate(own_key_grad.reshape(row_count, HK, HD), cosine, -sine)
        .reshape(row_count, HK * HD)
        .astype(bf16)
    )
    grad_value_lin = own_value_grad.reshape(row_count, HK * HD).astype(bf16)
    dw_query = jnp.einsum("rd,rf->df", first_in, grad_query_lin, preferred_element_type=f32)
    dw_key = jnp.einsum("rd,rf->df", first_in, grad_key_lin, preferred_element_type=f32)
    dw_value = jnp.einsum("rd,rf->df", first_in, grad_value_lin, preferred_element_type=f32)
    grad_first = (
        jnp.einsum("rf,df->rd", grad_query_lin, wq_back, preferred_element_type=f32)
        + jnp.einsum("rf,df->rd", grad_key_lin, wk_back, preferred_element_type=f32)
        + jnp.einsum("rf,df->rd", grad_value_lin, wv_back, preferred_element_type=f32)
    )
    grad_norm_one, dg_first = norm_back(x_rows, inverse_one, gain_first_b.astype(f32), grad_first)
    grad_in_rows = grad_middle + grad_norm_one
    shares = (
        lax.psum_scatter(
            dw_query.astype(jnp.bfloat16), "fsdp", scatter_dimension=0, tiled=True
        ).astype(jnp.float32),
        lax.psum_scatter(
            dw_key.astype(jnp.bfloat16), "fsdp", scatter_dimension=0, tiled=True
        ).astype(jnp.float32),
        lax.psum_scatter(
            dw_value.astype(jnp.bfloat16), "fsdp", scatter_dimension=0, tiled=True
        ).astype(jnp.float32),
        lax.psum_scatter(
            dw_out.astype(jnp.bfloat16), "fsdp", scatter_dimension=0, tiled=True
        ).astype(jnp.float32),
        lax.psum_scatter(
            dw_gate.astype(jnp.bfloat16), "fsdp", scatter_dimension=0, tiled=True
        ).astype(jnp.float32),
        lax.psum_scatter(
            dw_up.astype(jnp.bfloat16), "fsdp", scatter_dimension=0, tiled=True
        ).astype(jnp.float32),
        lax.psum_scatter(
            dw_down.astype(jnp.bfloat16), "fsdp", scatter_dimension=0, tiled=True
        ).astype(jnp.float32),
        lax.psum_scatter(
            dg_first.astype(jnp.bfloat16), "fsdp", scatter_dimension=0, tiled=True
        ).astype(jnp.float32),
        lax.psum_scatter(
            dg_second.astype(jnp.bfloat16), "fsdp", scatter_dimension=0, tiled=True
        ).astype(jnp.float32),
    )
    totals = lax.psum(
        (
            shares[0],
            shares[1],
            shares[2],
            shares[3],
            shares[4],
            shares[5],
            shares[6],
            shares[7],
            shares[8],
        ),
        "ctx",
    )
    return (
        result,
        grad_in_rows.reshape(hidden_in.shape),
        totals[0],
        totals[1],
        totals[2],
        totals[3],
        totals[4],
        totals[5],
        totals[6],
        totals[7],
        totals[8],
    )


def solution(mesh):
    in_specs = (
        P("fsdp", "ctx", None, None),
        P("fsdp", "ctx", None, None),
        P(),
        P("fsdp", "ctx", None),
        P("fsdp"),
        P("fsdp", None),
        P("fsdp", None),
        P("fsdp", None),
        P("fsdp", None),
        P("fsdp"),
        P("fsdp", None),
        P("fsdp", None),
        P("fsdp", None),
    )
    out_specs = (
        P("fsdp", "ctx", None, None),
        P("fsdp", "ctx", None, None),
        P("fsdp", None),
        P("fsdp", None),
        P("fsdp", None),
        P("fsdp", None),
        P("fsdp", None),
        P("fsdp", None),
        P("fsdp", None),
        P("fsdp"),
        P("fsdp"),
    )
    return jax.shard_map(shards, mesh=mesh, in_specs=in_specs, out_specs=out_specs, check_vma=False)
```

profile of v0, /device:TPU:0, one launch (start us, length us, event | category | flops | bytes accessed | tf_op | source)
XLA Modules:
  0.0 790.5 jit_solution(17607568749272585116)
XLA Ops:
  12.9 8.3 %all-reduce.6 = (bf16[576]{0:T(1024)(128)(2,1)S(1)}, bf16[576]{0:T(1024)(128)(2,1)S(1)}) all-reduce(bf16[576]{0:T(1024)(128)(2,1)S(1)} %dynamic-update-slice, bf16[576]{0:T(1024)(128)(2,1)S(1)} %dynamic-update-slice.1), channel_id=1, replica_groups=mesh['ctx'=8,'fsdp'=4] {'fsdp'}, use_global_device_ids=true, to_apply=%add | all-reduce | flops 1152 | bytes 4608
  21.2 6.1 all_gather.46
  32.9 6.0 all_gather.48
  45.6 8.4 %all_gather.45 = bf16[576,576]{1,0:T(8,128)(2,1)S(1)} all-gather(bf16[144,576]{1,0:T(8,128)(2,1)S(1)} %copy-done.33), channel_id=1, replica_groups=mesh['ctx'=8,'fsdp'=4] {'fsdp'}, dimensions={0}, use_global_device_ids=true | all-gather | bytes 829440 | tf_op jit(solution)/shard_map/all_gather | solution.py:76
  54.0 8.9 %all_gather.50 = bf16[576,576]{1,0:T(8,128)(2,1)} all-gather(bf16[144,576]{1,0:T(8,128)(2,1)S(1)} %copy-done.34), channel_id=1, replica_groups=mesh['ctx'=8,'fsdp'=4] {'fsdp'}, dimensions={0}, use_global_device_ids=true | all-gather | bytes 829440 | tf_op jit(solution)/shard_map/all_gather | solution.py:79
  64.4 12.8 %all-gather.6.cloned.1.call-done = bf16[2,2048,192]{1,2,0:T(8,128)(2,1)} async-done(((bf16[2,256,192]{1,2,0:T(8,128)(2,1)}), bf16[2,2048,192]{1,2,0:T(8,128)(2,1)}) %all-gather.6.cloned.1.call-update) | async-done | bytes 1572880 | tf_op jit(solution)/shard_map/all_gather | solution.py:107
  77.1 46.1 %all-gather.8.cloned.1.call-done = bf16[2,2048,192]{1,2,0:T(8,128)(2,1)} async-done(((bf16[2,256,192]{1,2,0:T(8,128)(2,1)}), bf16[2,2048,192]{1,2,0:T(8,128)(2,1)}) %all-gather.8.cloned.1.call-update) | async-done | bytes 1572880 | tf_op jit(solution)/shard_map/all_gather | solution.py:108
  123.3 39.3 %while.57 = (s32[]{:T(128)}, bf16[2,256,576]{1,2,0:T(8,128)(2,1)}, f32[2,3,3,256]{3,2,1,0:T(4,128)S(1)}, bf16[2,256,3,3,64]{1,4,3,2,0:T(8,128)(2,1)S(1)}, bf16[2...) while((s32[]{:T(128)}, bf16[2,256,576]{1,2,0:T(8,128)(2,1)}, ...), condition=%wide.region_6.7_spmd.clone, body=%wide.region_1.6_spmd.clone.sunk | while | flops 422100224 | bytes 26083628 | solution.py:134
  125.5 15.9 %while.60 = (s32[]{:T(128)}, bf16[3,256,3,64]{1,3,2,0:T(8,128)(2,1)}, f32[3,3,256]{2,1,0:T(4,128)S(1)}, bf16[3,2048,64]{1,2,0:T(8,128)(2,1)S(1)}, pred[1,256,204...) while((s32[]{:T(128)}, ...), condition=%wide.region_5.5_spmd, body=%wide.region_2.4_spmd.sunk | while | flops 421575936 | bytes 21199968 | solution.py:129
  145.0 15.8 %while.60 = (s32[]{:T(128)}, bf16[3,256,3,64]{1,3,2,0:T(8,128)(2,1)}, f32[3,3,256]{2,1,0:T(4,128)S(1)}, bf16[3,2048,64]{1,2,0:T(8,128)(2,1)S(1)}, pred[1,256,204...) while((s32[]{:T(128)}, ...), condition=%wide.region_5.5_spmd, body=%wide.region_2.4_spmd.sunk | while | flops 421575936 | bytes 21199968 | solution.py:129
  176.4 11.8 %all-gather.14.cloned.1.call-done = bf16[1536,576]{0,1:T(8,128)(2,1)} async-done(((bf16[384,576]{0,1:T(8,128)(2,1)}), bf16[1536,576]{0,1:T(8,128)(2,1)}) %all-gather.14.cloned.1.call-update) | async-done | bytes 1769488 | tf_op jit(solution)/shard_map/all_gather | solution.py:82
  188.2 6.2 multiply_convert_fusion
  204.0 102.0 %while.59 = (s32[]{:T(128)}, f32[2,256,576]{1,0,2:T(2,128)}, f32[2,2048,192]{1,2,0:T(8,128)}, f32[2,2048,192]{1,2,0:T(8,128)}, bf16[2,256,3,3,64]{1,4,3,2,0:T(8,...) while((s32[]{:T(128)}, f32[2,256,576]{1,0,2:T(2,128)}, ...), condition=%wide.region_13.14_spmd.clone, body=%wide.region_9.13_spmd.clone.sunk | while | flops 1021492480 | bytes 82559448 | solution.py:230
  207.9 29.3 %while.61 = (s32[]{:T(128)}, f32[3,256,3,64]{1,3,2,0:T(8,128)}, f32[3,2048,64]{1,2,0:T(8,128)}, f32[3,2048,64]{1,2,0:T(8,128)}, bf16[3,2048,64]{1,2,0:T(8,128)(2...) while((s32[]{:T(128)}, f32[3,256,3,64]{1,3,2,0:T(8,128)}, ...), condition=%wide.region_12.12_spmd, body=%wide.region_10.11_spmd.sunk | while | flops 1020968192 | bytes 62739632 | solution.py:214
  239.1 12.7 %dynamic_update_slice.64 = f32[2,256,576]{1,0,2:T(2,128)} dynamic-update-slice(f32[2,256,576]{1,0,2:T(2,128)} %get-tuple-element.827, f32[1,256,576]{1,0,2:T(1,128)S(1)} %copy.108, s32[]{:T(128)S(6)} %copy.156, s32[]{:T(128)} %constant.123.clone.1..sunk.1, s32[]{:T(128)} %constant.123.clone.1..sunk.1) | dynamic-update-slice | bytes 1179652 | tf_op jit(solution)/shard_map/while/body/jit(dynamic_update_index_in_dim)/dynamic_update_slice | solution.py:230
  259.0 29.3 %while.61 = (s32[]{:T(128)}, f32[3,256,3,64]{1,3,2,0:T(8,128)}, f32[3,2048,64]{1,2,0:T(8,128)}, f32[3,2048,64]{1,2,0:T(8,128)}, bf16[3,2048,64]{1,2,0:T(8,128)(2...) while((s32[]{:T(128)}, f32[3,256,3,64]{1,3,2,0:T(8,128)}, ...), condition=%wide.region_12.12_spmd, body=%wide.region_10.11_spmd.sunk | while | flops 1020968192 | bytes 62739632 | solution.py:214
  290.1 12.7 %dynamic_update_slice.64 = f32[2,256,576]{1,0,2:T(2,128)} dynamic-update-slice(f32[2,256,576]{1,0,2:T(2,128)} %get-tuple-element.827, f32[1,256,576]{1,0,2:T(1,128)S(1)} %copy.108, s32[]{:T(128)S(6)} %copy.156, s32[]{:T(128)} %constant.123.clone.1..sunk.1, s32[]{:T(128)} %constant.123.clone.1..sunk.1) | dynamic-update-slice | bytes 1179652 | tf_op jit(solution)/shard_map/while/body/jit(dynamic_update_index_in_dim)/dynamic_update_slice | solution.py:230
  338.0 29.4 %reduce-scatter.28.cloned.1.call-done = bf16[384,576]{1,0:T(8,128)(2,1)} async-done(((bf16[1536,576]{1,0:T(8,128)(2,1)}), bf16[384,576]{1,0:T(8,128)(2,1)}) %reduce-scatter.28.cloned.1.call-update) | async-done | bytes 442384
  369.3 30.2 %reduce-scatter.24.cloned.1.call-done = bf16[144,1536]{1,0:T(8,128)(2,1)} async-done(((bf16[576,1536]{1,0:T(8,128)(2,1)}), bf16[144,1536]{1,0:T(8,128)(2,1)}) %reduce-scatter.24.cloned.1.call-update) | async-done | bytes 442384 | tf_op jit(solution)/shard_map/reduce_scatter | solution.py:271
  399.5 31.8 %reduce-scatter.26.cloned.1.call-done = bf16[144,1536]{1,0:T(8,128)(2,1)} async-done(((bf16[576,1536]{1,0:T(8,128)(2,1)}), bf16[144,1536]{1,0:T(8,128)(2,1)}) %reduce-scatter.26.cloned.1.call-update) | async-done | bytes 442384 | tf_op jit(solution)/shard_map/reduce_scatter | solution.py:274
  431.3 78.9 %reduce-scatter.14.cloned.1.call-done = f32[2,256,192]{1,2,0:T(8,128)} async-done(((f32[2,2048,192]{1,2,0:T(8,128)}), f32[2,256,192]{1,2,0:T(8,128)}) %reduce-scatter.14.cloned.1.call-update) | async-done | bytes 393232 | tf_op jit(solution)/shard_map/reduce_scatter | solution.py:235
  511.9 76.3 %reduce-scatter.12.cloned.1.call-done = f32[2,256,192]{1,2,0:T(8,128)} async-done(((f32[2,2048,192]{1,2,0:T(8,128)}), f32[2,256,192]{1,2,0:T(8,128)}) %reduce-scatter.12.cloned.1.call-update) | async-done | bytes 393232 | tf_op jit(solution)/shard_map/reduce_scatter | solution.py:234
  611.0 23.2 %reduce-scatter.20.cloned.1.call-done = bf16[144,192]{1,0:T(8,128)(2,1)} async-done(((bf16[576,192]{1,0:T(8,128)(2,1)}), bf16[144,192]{1,0:T(8,128)(2,1)}) %reduce-scatter.20.cloned.1.call-update) | async-done | bytes 55312 | tf_op jit(solution)/shard_map/reduce_scatter | solution.py:265
  634.2 149.3 %all-reduce.8 = (f32[144,576]{1,0:T(8,128)}, f32[144,192]{1,0:T(8,128)}, f32[144,192]{1,0:T(8,128)}, f32[144,576]{1,0:T(8,128)}, f32[144,1536]{1,0:T(8,128)}, /*...) all-reduce(bf16[144,576]{1,0:T(8,128)(2,1)S(1)} %copy-done.36, ...), channel_id=1, replica_groups=mesh['ctx'=8,'fsdp'=4] {'ctx'}, use_global_device_ids=true, to_apply=%region_18.19 | all-reduce | flops 885024 | bytes 5310720 | tf_op jit(solution)/shard_map/psum | solution.py:287
  (346 shorter events, 214.4 us)
Async XLA Ops:
  7.2 20.8 %copy-start.13 = (bf16[2,1,256,576]{2,3,1,0:T(8,128)(2,1)S(1)}, bf16[2,1,256,576]{2,3,1,0:T(8,128)(2,1)}, u32[]{:S(2)}) copy-start(bf16[2,1,256,576]{2,3,1,0:T(8,128)(2,1)} %param.21) | copy-start | bytes 1769476
  7.2 70.0 %all-gather.6.cloned.1.call-start = ((), (), s32[]{:S(2)}) async-start(), calls=%async_computation.9 | async-start | bytes 1769472 | tf_op jit(solution)/shard_map/all_gather | solution.py:107
  21.2 17.7 %copy-start.37 = (f32[576]{0:T(1024)}, f32[576]{0:T(1024)S(1)}, u32[]{:S(2)}) copy-start(f32[576]{0:T(1024)S(1)} %convert_element_type.184) | copy-start | bytes 6916
  30.1 33.7 %copy-start.25 = (f32[512,32]{0,1:T(8,128)}, f32[512,32]{0,1:T(8,128)S(1)}, u32[]{:S(2)}) copy-start(f32[512,32]{0,1:T(8,128)S(1)} %get-tuple-element.427) | copy-start | bytes 196612
  31.3 92.0 %all-gather.8.cloned.1.call-start = ((), (), s32[]{:S(2)}) async-start(), calls=%async_computation.10 | async-start | bytes 1769472 | tf_op jit(solution)/shard_map/all_gather | solution.py:108
  40.3 125.7 %all-gather.12.cloned.1.call-start = ((), (), s32[]{:S(2)}) async-start(), calls=%async_computation.12 | async-start | bytes 2211840 | tf_op jit(solution)/shard_map/all_gather | solution.py:81
  41.1 130.6 %all-gather.10.cloned.1.call-start = ((), (), s32[]{:S(2)}) async-start(), calls=%async_computation.11 | async-start | bytes 2211840 | tf_op jit(solution)/shard_map/all_gather | solution.py:80
  41.7 146.6 %all-gather.14.cloned.1.call-start = ((), (), s32[]{:S(2)}) async-start(), calls=%async_computation.13 | async-start | bytes 2211840 | tf_op jit(solution)/shard_map/all_gather | solution.py:82
  42.2 295.7 %reduce-scatter.22.cloned.1.call-start = ((), (), s32[]{:S(2)}) async-start(), calls=%async_computation.19 | async-start | bytes 921600 | tf_op jit(solution)/shard_map/reduce_scatter | solution.py:268
  165.8 33.2 %copy-start.8 = (f32[512,576]{0,1:T(8,128)}, f32[512,576]{0,1:T(8,128)S(1)}, u32[]{:S(2)}) copy-start(f32[512,576]{0,1:T(8,128)S(1)} %get-tuple-element.435) | copy-start | bytes 3538948
  171.6 16.6 %copy-start.19 = (bf16[72,8,2,256]{3,1,2,0:T(8,128)(2,1)S(1)}, bf16[72,8,2,256]{3,1,2,0:T(8,128)(2,1)}, u32[]{:S(2)}) copy-start(bf16[72,8,2,256]{3,1,2,0:T(8,128)(2,1)} %copy.101) | copy-start | bytes 1769476
  203.7 134.2 %reduce-scatter.16.cloned.1.call-start = ((), (), s32[]{:S(2)}) async-start(), calls=%async_computation.16 | async-start | bytes 921600 | tf_op jit(solution)/shard_map/reduce_scatter | solution.py:259
  310.9 56.4 %reduce-scatter.28.cloned.1.call-start = ((), (), s32[]{:S(2)}) async-start(), calls=%async_computation.22 | async-start | bytes 2457600
  318.6 80.9 %reduce-scatter.24.cloned.1.call-start = ((), (), s32[]{:S(2)}) async-start(), calls=%async_computation.20 | async-start | bytes 2211840 | tf_op jit(solution)/shard_map/reduce_scatter | solution.py:271
  323.4 107.9 %reduce-scatter.26.cloned.1.call-start = ((), (), s32[]{:S(2)}) async-start(), calls=%async_computation.21 | async-start | bytes 2211840 | tf_op jit(solution)/shard_map/reduce_scatter | solution.py:274
  327.2 183.0 %reduce-scatter.14.cloned.1.call-start = ((), (), s32[]{:S(2)}) async-start(), calls=%async_computation.15 | async-start | bytes 3538944 | tf_op jit(solution)/shard_map/reduce_scatter | solution.py:235
  327.9 260.4 %reduce-scatter.12.cloned.1.call-start = ((), (), s32[]{:S(2)}) async-start(), calls=%async_computation.14 | async-start | bytes 3538944 | tf_op jit(solution)/shard_map/reduce_scatter | solution.py:234
  328.5 282.5 %reduce-scatter.18.cloned.1.call-start = ((), (), s32[]{:S(2)}) async-start(), calls=%async_computation.17 | async-start | bytes 368640 | tf_op jit(solution)/shard_map/reduce_scatter | solution.py:262
  591.1 43.1 %reduce-scatter.20.cloned.1.call-start = ((), (), s32[]{:S(2)}) async-start(), calls=%async_computation.18 | async-start | bytes 368640 | tf_op jit(solution)/shard_map/reduce_scatter | solution.py:265
  599.5 34.8 %copy-start.23 = (bf16[384,576]{0,1:T(8,128)(2,1)S(1)}, bf16[384,576]{0,1:T(8,128)(2,1)}, u32[]{:S(2)}) copy-start(bf16[384,576]{0,1:T(8,128)(2,1)} %copy.86) | copy-start | bytes 1327108
  599.5 34.7 %copy-start.31 = (bf16[144,1536]{1,0:T(8,128)(2,1)S(1)}, bf16[144,1536]{1,0:T(8,128)(2,1)}, u32[]{:S(2)}) copy-start(bf16[144,1536]{1,0:T(8,128)(2,1)} %reduce-scatter.24.cloned.1.call-done) | copy-start | bytes 1327108
  599.5 34.7 %copy-start.32 = (bf16[144,1536]{1,0:T(8,128)(2,1)S(1)}, bf16[144,1536]{1,0:T(8,128)(2,1)}, u32[]{:S(2)}) copy-start(bf16[144,1536]{1,0:T(8,128)(2,1)} %reduce-scatter.26.cloned.1.call-done) | copy-start | bytes 1327108
  599.5 34.7 %copy-start.35 = (bf16[144,576]{1,0:T(8,128)(2,1)S(1)}, bf16[144,576]{1,0:T(8,128)(2,1)}, u32[]{:S(2)}) copy-start(bf16[144,576]{1,0:T(8,128)(2,1)} %reduce-scatter.22.cloned.1.call-done) | copy-start | bytes 497668
  599.5 34.7 %copy-start.36 = (bf16[144,576]{1,0:T(8,128)(2,1)S(1)}, bf16[144,576]{1,0:T(8,128)(2,1)}, u32[]{:S(2)}) copy-start(bf16[144,576]{1,0:T(8,128)(2,1)} %reduce-scatter.16.cloned.1.call-done) | copy-start | bytes 497668
  (50 other events, 139.6 us)
Sparse Core Ops, SparseCore 0:
  31.4 45.6 all-gather.5
  79.8 43.4 all-gather.7
  124.8 18.9 all-gather.11
  145.2 20.7 all-gather.9
  167.4 20.7 all-gather.13
  203.9 22.9 reduce-scatter.21
  311.0 22.9 reduce-scatter.15
  336.6 30.6 reduce-scatter.27
  370.1 29.3 reduce-scatter.23
  401.9 29.3 reduce-scatter.25
  435.4 74.8 reduce-scatter.13
  514.1 74.1 reduce-scatter.11
  591.5 19.4 reduce-scatter.17
  613.9 20.2 reduce-scatter.19
where the time goes:
time: 800 us; the launch traced here: 791 us
  waiting for transfers between devices  348 us (44%)
  blocking collectives  193 us (24%)
  matrix products  116 us (14%)
  local copies, waits for them, and re-layouts  90.6 us (11%)
  other arithmetic  25.4 us (3%)
  between operations  16.4 us (2%)
    psum x1, blocking collectives, shards(): lax.psum((shares[0], shares[1], shares[2], shares[3], shares[4], shares[5...  149 us
    reduce_scatter x1, waiting for transfers between devices, shards(): lax.psum_scatter(grad_value_seqs, 'ctx', scatter_dimension=1, tiled=True)  78.9 us
    reduce_scatter x1, waiting for transfers between devices, shards(): lax.psum_scatter(grad_key_seqs, 'ctx', scatter_dimension=1, tiled=True)  76.3 us
    all_gather x1, waiting for transfers between devices, shards(): lax.all_gather(outgoing[1], 'ctx', axis=1, tiled=True)  46.1 us
    dynamic_update_slice x6, local copies, waits for them, and re-layouts, shards(): lax.map(backward_seq, (query_seqs, keys_back, values_back, grad_mixed_seq...  35.5 us
    unnamed x15, waiting for transfers between devices  32.4 us
    reduce_scatter x1, waiting for transfers between devices, shards(): lax.psum_scatter(dw_up.astype(jnp.bfloat16), 'fsdp', scatter_dimension=0,...  31.8 us
    reduce_scatter x1, waiting for transfers between devices, shards(): lax.psum_scatter(dw_gate.astype(jnp.bfloat16), 'fsdp', scatter_dimension=...  30.2 us
  transfers between devices with their start and end apart: 14, of which 10 were waited for; matrix products, arithmetic and copies ran while one was open for 24% of the time, Pallas kernels for 0%

commit v1 on v0

v1 whole, which is shorter than its diff:
```python
import functools
import math

import jax
import jax.numpy as jnp
from jax import lax
from jax.experimental import pallas as pl
from jax.experimental.pallas import tpu as pltpu
from jax.sharding import PartitionSpec as P

HQ = 9
HK = 3
HD = 64


EPS = 1e-05
THETA = 100000.0


def rotate(vector, cosine, sine):
    half_dim = vector.shape[-1] // 2
    first = vector[..., :half_dim]
    second = vector[..., half_dim:]
    return jnp.concatenate(
        [first * cosine - second * sine, second * cosine + first * sine], axis=-1
    )


def rope_tables(place, head_dim):
    half_dim = head_dim // 2
    inverse = jnp.exp(jnp.arange(half_dim, dtype=jnp.float32) * (-math.log(THETA) / half_dim))
    angles = place.astype(jnp.float32)[:, None] * inverse[None, :]
    return (jnp.cos(angles)[:, None, :], jnp.sin(angles)[:, None, :])


def norm_back(vector, inverse, gain_vec, incoming):
    scaled = incoming * gain_vec
    gain_grad = jnp.sum(incoming * vector * inverse, axis=0)
    vector_grad = inverse * scaled - vector * (inverse * inverse * inverse) * jnp.mean(
        scaled * vector, axis=-1, keepdims=True
    )
    return (vector_grad, gain_grad)


MESH = pl.DeviceIdType.MESH
VMEM = pltpu.VMEM
BIG = 56 * 1024 * 1024


def ring_pos(index, count):
    odd = lax.rem(index, 2)
    return (1 - odd) * (index // 2) + odd * (count - 1 - index // 2)


def ring_index(place, count):
    place = lax.rem(place + 2 * count, count)
    back = place // (count // 2)
    return (1 - back) * (2 * place) + back * (2 * (count - 1 - place) + 1)


def neighbours(count):
    me = lax.axis_index("ctx")
    shard = lax.axis_index("fsdp")
    place = ring_pos(me, count)
    core = shard + 1 - 2 * lax.rem(shard, 2)
    across = lax.rem(shard + 2, 4)
    right = (ring_index(place + 1, count), shard)
    left = (ring_index(place - 1, count), shard)
    return me, shard, place, (me, core), (me, across), right, left


def greet(partners):
    barrier = pltpu.get_barrier_semaphore()
    for partner in partners:
        pl.semaphore_signal(barrier, inc=1, device_id=partner, device_id_type=MESH)
    pl.semaphore_wait(barrier, len(partners))


def remote(source, target, send, recv, device):
    return pltpu.make_async_remote_copy(
        src_ref=source,
        dst_ref=target,
        send_sem=send,
        recv_sem=recv,
        device_id=device,
        device_id_type=MESH,
    )


def comm_call(kernel, out_shape, scratch, cid, args):
    vm = pl.BlockSpec(memory_space=VMEM)
    return pl.pallas_call(
        kernel,
        out_shape=out_shape,
        in_specs=[vm] * len(args),
        out_specs=[vm] * len(out_shape),
        scratch_shapes=scratch,
        compiler_params=pltpu.CompilerParams(
            collective_id=cid, has_side_effects=True, vmem_limit_bytes=BIG
        ),
    )(*args)


class WeightGather:
    def __init__(self, ins, outs, sems, base, shard, core, across):
        self.parts = []
        for k, (src, dst) in enumerate(zip(ins, outs)):
            rows = src.shape[0]

            def slot(owner, dst=dst, rows=rows):
                return dst.at[pl.ds(pl.multiple_of(owner * rows, 16), rows)]

            other_core = shard + 1 - 2 * lax.rem(shard, 2)
            over = lax.rem(shard + 2, 4)
            sem = lambda j, k=k: (sems.at[0, base + k, j], sems.at[1, base + k, j])
            cross = remote(src, slot(shard), *sem(0), across)
            near = remote(src, slot(shard), *sem(1), core)
            onward = remote(slot(over), slot(over), *sem(2), core)
            self.parts.append((cross, near, onward, src, dst, shard, rows))

    def start(self):
        for cross, near, *_ in self.parts:
            cross.start()
            near.start()
        for _, _, _, src, dst, shard, rows in self.parts:
            dst[pl.ds(pl.multiple_of(shard * rows, 16), rows)] = src[...]

    def forward(self):
        for cross, _, onward, *_ in self.parts:
            cross.wait_recv()
            onward.start()

    def finish(self):
        for cross, near, onward, *_ in self.parts:
            near.wait_recv()
            onward.wait_recv()
            cross.wait_send()
            near.wait_send()
            onward.wait_send()


def gather_small(count, *refs):
    k = (len(refs) - 1) // 2
    ins, outs, sems = refs[:k], refs[k : 2 * k], refs[-1]
    _, shard, _, core, across, _, _ = neighbours(count)
    greet((core, across))
    work = WeightGather(ins, outs, sems, 0, shard, core, across)
    work.start()
    work.forward()
    work.finish()


def gather_weights(count, arrays, cid):
    outs = [jax.ShapeDtypeStruct((4 * a.shape[0], a.shape[1]), a.dtype) for a in arrays]
    return comm_call(
        functools.partial(gather_small, count),
        outs,
        [pltpu.SemaphoreType.DMA((2, len(arrays), 3))],
        cid,
        arrays,
    )


def gather_both_kernel(count, kv_ref, *refs):
    k = (len(refs) - 3) // 2
    ins, all_ref, outs = refs[:k], refs[k], refs[k + 1 : 2 * k + 1]
    sems, ring = refs[-2:]
    me, shard, place, core, across, right, left = neighbours(count)
    greet((core, across, right, left))
    half = count // 2
    rows = kv_ref.shape[0]

    def step(t, way):
        block = ring_index(place - way * (t - 1), count)
        src = kv_ref if t == 1 else all_ref.at[block]
        dst = all_ref.at[block]
        if t == half:
            cut = pl.ds(0, rows // 2) if way > 0 else pl.ds(rows // 2, rows // 2)
            src, dst = src.at[cut], dst.at[cut]
        lane = 0 if way > 0 else 1
        return remote(
            src, dst, ring.at[0, lane, t - 1], ring.at[1, lane, t - 1], right if way > 0 else left
        )

    steps = [(step(t, 1), step(t, -1)) for t in range(1, half + 1)]
    steps[0][0].start()
    steps[0][1].start()
    work = WeightGather(ins, outs, sems, 0, shard, core, across)
    work.start()
    all_ref[me] = kv_ref[...]
    for t in range(1, half):
        for way in (0, 1):
            steps[t - 1][way].wait_recv()
            steps[t][way].start()
    work.forward()
    for way in (0, 1):
        steps[half - 1][way].wait_recv()
    for pair in steps:
        pair[0].wait_send()
        pair[1].wait_send()
    work.finish()


def gather_both(count, kv, arrays, cid):
    outs = [jax.ShapeDtypeStruct((count,) + kv.shape, kv.dtype)]
    outs += [jax.ShapeDtypeStruct((4 * a.shape[0], a.shape[1]), a.dtype) for a in arrays]
    return comm_call(
        functools.partial(gather_both_kernel, count),
        outs,
        [
            pltpu.SemaphoreType.DMA((2, len(arrays), 3)),
            pltpu.SemaphoreType.DMA((2, 2, count // 2)),
        ],
        cid,
        [kv] + list(arrays),
    )


def add_rows(rows, block, body):
    def one(i, carry):
        body(pl.ds(pl.multiple_of(i * block, 16), block))
        return carry

    lax.fori_loop(0, rows // block, one, 0)


class ShardSum:
    def __init__(self, pack, out, near_buf, far_buf, sems, chunks, shard, core, across):
        self.pack, self.out, self.near_buf, self.far_buf = pack, out, near_buf, far_buf
        self.size = pack.shape[1] // chunks
        self.chunks = chunks
        self.mine, self.side = lax.rem(shard, 2), shard // 2
        self.near, self.far = [], []
        for c in range(chunks):
            cut = pl.ds(c * self.size, self.size)
            pair = []
            for x in range(2):
                pair.append(
                    remote(
                        pack.at[2 * x + 1 - self.mine, cut],
                        near_buf.at[x, cut],
                        sems.at[0, c, x],
                        sems.at[1, c, x],
                        core,
                    )
                )
            self.near.append(pair)
            self.far.append(
                remote(
                    near_buf.at[1 - self.side, cut],
                    far_buf.at[cut],
                    sems.at[0, c, 2],
                    sems.at[1, c, 2],
                    across,
                )
            )

    def start(self):
        for pair in self.near:
            for copy in pair:
                copy.start()

    def cross(self, c):
        for copy in self.near[c]:
            copy.wait_recv()

        def body(cut):
            for x in (0, 1):
                total = self.pack[2 * x + self.mine, cut].astype(jnp.float32) + self.near_buf[
                    x, cut
                ].astype(jnp.float32)
                self.near_buf[x, cut] = total.astype(jnp.bfloat16)

        base = c * self.size
        add_rows(self.size, 16, lambda cut: body(pl.ds(pl.multiple_of(base + cut.start, 16), cut.size)))
        self.far[c].start()

    def close(self, c):
        self.far[c].wait_recv()
        self.far[c].wait_send()

        def body(cut):
            total = self.near_buf[self.side, cut].astype(jnp.float32) + self.far_buf[cut].astype(
                jnp.float32
            )
            self.out[cut] = total.astype(jnp.bfloat16)

        base = c * self.size
        add_rows(self.size, 16, lambda cut: body(pl.ds(pl.multiple_of(base + cut.start, 16), cut.size)))

    def finish(self):
        for pair in self.near:
            for copy in pair:
                copy.wait_send()


class RingSum:
    def __init__(self, count, term, rows, cuts, send_buf, recv_buf, sems, place, right, left):
        self.count, self.term, self.rows, self.cuts = count, term, rows, cuts
        self.send_buf, self.recv_buf, self.place = send_buf, recv_buf, place
        self.half = count // 2
        self.copies = []
        for t in range(self.half):
            pair = []
            for lane in (0, 1):
                src, dst = send_buf.at[lane, t], recv_buf.at[lane, t]
                if t == 0:
                    src, dst = src.at[cuts[lane]], dst.at[cuts[lane]]
                pair.append(
                    remote(
                        src, dst, sems.at[0, lane, t], sems.at[1, lane, t], left if lane else right
                    )
                )
            self.copies.append(pair)

    def piece(self, t, lane):
        away = self.half - t
        return ring_index(self.place + (away if lane == 0 else -away), self.count)

    def start(self):
        for lane in (0, 1):
            index = self.piece(0, lane)
            cut = self.cuts[lane]
            self.send_buf[(lane, 0) + cut] = self.term(index)[cut]
            self.copies[0][lane].start()

    def step(self, t):
        for lane in (0, 1):
            self.copies[t - 1][lane].wait_recv()
            index = self.piece(t, lane)
            own = self.term(index)
            if t == 1:
                cut, rest = self.cuts[lane], self.cuts[1 - lane]
                self.send_buf[(lane, t) + rest] = own[rest]
                total = own[cut].astype(jnp.float32) + self.recv_buf[(lane, 0) + cut].astype(
                    jnp.float32
                )
                self.send_buf[(lane, t) + cut] = total.astype(jnp.bfloat16)
            else:

                def body(cut):
                    total = own[cut].astype(jnp.float32) + self.recv_buf[lane, t - 1, cut].astype(
                        jnp.float32
                    )
                    self.send_buf[lane, t, cut] = total.astype(jnp.bfloat16)

                add_rows(self.rows, 16, body)
            self.copies[t][lane].start()

    def last(self, store):
        for lane in (0, 1):
            self.copies[self.half - 1][lane].wait_recv()
        own = self.term(ring_index(self.place, self.count))

        def body(cut):
            total = (
                own[cut].astype(jnp.float32)
                + self.recv_buf[0, self.half - 1, cut].astype(jnp.float32)
                + self.recv_buf[1, self.half - 1, cut].astype(jnp.float32)
            )
            store(cut, total)

        add_rows(self.rows, 16, body)

    def finish(self):
        for pair in self.copies:
            for copy in pair:
                copy.wait_send()


def kv_back_kernel(
    count, chunks, dkv, pack, own_ref, sum_ref, near_buf, far_buf, sends, recvs, sems, ring
):
    me, shard, place, core, across, right, left = neighbours(count)
    greet((core, across, right, left))
    half = count // 2
    rows = dkv.shape[1]
    cuts = ((pl.ds(0, rows // 2),), (pl.ds(rows // 2, rows // 2),))
    turn = RingSum(count, lambda i: dkv.at[i], rows, cuts, sends, recvs, ring, place, right, left)
    turn.start()
    shares = ShardSum(pack, sum_ref, near_buf, far_buf, sems, chunks, shard, core, across)
    shares.start()
    for c in range(chunks):
        shares.cross(c)
    for t in range(1, half):
        turn.step(t)

    def store(cut, total):
        own_ref[cut] = total

    for c in range(chunks):
        shares.close(c)
    turn.last(store)
    turn.finish()
    shares.finish()


def kv_back(count, dkv, pack, cid):
    _, rows, width = dkv.shape
    _, prow, pwid = pack.shape
    chunks = 4
    bf16 = jnp.bfloat16
    half = count // 2
    return comm_call(
        functools.partial(kv_back_kernel, count, chunks),
        [
            jax.ShapeDtypeStruct((rows, width), jnp.float32),
            jax.ShapeDtypeStruct((prow, pwid), bf16),
        ],
        [
            VMEM((2, prow, pwid), bf16),
            VMEM((prow, pwid), bf16),
            VMEM((2, half, rows, width), bf16),
            VMEM((2, half, rows, width), bf16),
            pltpu.SemaphoreType.DMA((2, chunks, 3)),
            pltpu.SemaphoreType.DMA((2, 2, half)),
        ],
        cid,
        [dkv, pack],
    )


class RingGather:
    def __init__(self, count, out, rows, cuts, sems, place, right, left):
        half = count // 2
        self.copies = []
        for t in range(half):
            pair = []
            for lane in (0, 1):
                index = ring_index(place - t if lane == 0 else place + t, count)
                cut = (pl.ds(pl.multiple_of(index * rows, 16), rows),)
                if t == half - 1:
                    cut += cuts[lane][1:]
                pair.append(
                    remote(
                        out.at[cut],
                        out.at[cut],
                        sems.at[0, lane, t],
                        sems.at[1, lane, t],
                        left if lane else right,
                    )
                )
            self.copies.append(pair)

    def start(self):
        for copy in self.copies[0]:
            copy.start()

    def step(self, t):
        for lane in (0, 1):
            self.copies[t - 1][lane].wait_recv()
            self.copies[t][lane].start()

    def finish(self):
        for copy in self.copies[-1]:
            copy.wait_recv()
        for pair in self.copies:
            for copy in pair:
                copy.wait_send()


def ring_parts(count, source, out, sends, recvs, sems_sum, sems_all, place, right, left):
    rows, width = source.shape[0] // count, source.shape[1]
    cuts = ((slice(None), pl.ds(0, width // 2)), (slice(None), pl.ds(width // 2, width // 2)))
    term = lambda i: source.at[pl.ds(pl.multiple_of(i * rows, 16), rows)]
    turn = RingSum(count, term, rows, cuts, sends, recvs, sems_sum, place, right, left)
    spread = RingGather(count, out, rows, cuts, sems_all, place, right, left)
    base = ring_index(place, count) * rows

    def store(cut, total):
        out[pl.ds(pl.multiple_of(base + cut.start, 16), cut.size)] = total.astype(jnp.bfloat16)

    return turn, spread, store


def last_sum_kernel(
    count, part, pack, out_f, out_q, near_buf, far_buf, sum_q,
    sf, rf, sq, rq, sems, ra, rb, rc, rd,
):
    me, shard, place, core, across, right, left = neighbours(count)
    greet((core, across, right, left))
    half = count // 2
    shares = ShardSum(pack, sum_q, near_buf, far_buf, sems, 1, shard, core, across)
    shares.start()
    turn_f, spread_f, store_f = ring_parts(
        count, part, out_f, sf, rf, ra, rb, place, right, left
    )
    turn_q, spread_q, store_q = ring_parts(
        count, sum_q, out_q, sq, rq, rc, rd, place, right, left
    )
    turn_f.start()
    shares.cross(0)
    if half > 1:
        turn_f.step(1)
    shares.close(0)
    turn_q.start()
    for t in range(2, half + 1):
        if t < half:
            turn_f.step(t)
        turn_q.step(t - 1)
    turn_f.last(store_f)
    spread_f.start()
    turn_q.last(store_q)
    spread_q.start()
    for t in range(1, half):
        spread_f.step(t)
        spread_q.step(t)
    spread_f.finish()
    spread_q.finish()
    turn_f.finish()
    turn_q.finish()
    shares.finish()


def last_sum(count, part, pack, cid):
    frow, fwid = part.shape
    _, qrow, qwid = pack.shape
    bf16 = jnp.bfloat16
    half = count // 2
    dma = pltpu.SemaphoreType.DMA
    return comm_call(
        functools.partial(last_sum_kernel, count),
        [jax.ShapeDtypeStruct((frow, fwid), bf16), jax.ShapeDtypeStruct((qrow, qwid), bf16)],
        [
            VMEM((2, qrow, qwid), bf16),
            VMEM((qrow, qwid), bf16),
            VMEM((qrow, qwid), bf16),
            VMEM((2, half, frow // count, fwid), bf16),
            VMEM((2, half, frow // count, fwid), bf16),
            VMEM((2, half, qrow // count, qwid), bf16),
            VMEM((2, half, qrow // count, qwid), bf16),
            dma((2, 1, 3)),
            dma((2, 2, half)),
            dma((2, 2, half)),
            dma((2, 2, half)),
            dma((2, 2, half)),
        ],
        cid,
        [part, pack],
    )


def shards(
    hidden_in,
    cotangent,
    span_table,
    positions,
    attn_gain,
    w_query,
    w_key,
    w_value,
    w_out,
    ffn_gain,
    w_gate,
    w_up,
    w_down,
):
    seq_count = hidden_in.shape[0]
    pair_rows = hidden_in.shape[2]
    width = hidden_in.shape[3]
    span_rows = pair_rows // 2
    ctx_count = lax.axis_size("ctx")
    full_len = ctx_count * pair_rows
    row_count = seq_count * pair_rows
    group_size = HQ // HK
    score_scale = 1.0 / math.sqrt(HD)
    f32 = jnp.float32
    bf16 = jnp.bfloat16
    columns = jnp.arange(pair_rows, dtype=jnp.int32)
    span_ids = jnp.where(
        columns[None, :] < span_rows, span_table[:, None], 2 * ctx_count - 1 - span_table[:, None]
    )
    key_order = (span_ids * span_rows + columns[None, :] % span_rows).reshape(full_len)
    own_order = lax.dynamic_slice_in_dim(key_order, lax.axis_index("ctx") * pair_rows, pair_rows)
    allowed = (key_order[None, :] <= own_order[:, None])[None, :, :]
    gains_own = jnp.concatenate(
        [attn_gain[None], ffn_gain[None], jnp.zeros((14,) + attn_gain.shape, bf16)], axis=0
    )
    qkv_all, gains_all = gather_weights(
        ctx_count, [jnp.concatenate([w_query, w_key, w_value], axis=1), gains_own], 0
    )
    gains_all = gains_all.reshape(4, 16, -1)
    gain_first = gains_all[:, 0].reshape(width)
    gain_second = gains_all[:, 1].reshape(width)
    cosine, sine = rope_tables(positions.reshape(row_count), HD)
    x_rows = hidden_in.reshape(row_count, width).astype(f32)
    inverse_one = lax.rsqrt(jnp.mean(x_rows * x_rows, axis=-1, keepdims=True) + EPS)
    first_in = (x_rows * inverse_one * gain_first.astype(f32)).astype(bf16)
    qkv_rows = jnp.dot(first_in, qkv_all, preferred_element_type=f32)
    q_width, k_width = HQ * HD, HK * HD
    query_rows = rotate(
        qkv_rows[:, :q_width].reshape(row_count, HQ, HD), cosine, sine
    ).astype(bf16)
    key_rows = rotate(
        qkv_rows[:, q_width : q_width + k_width].reshape(row_count, HK, HD), cosine, sine
    ).astype(bf16)
    value_rows = qkv_rows[:, q_width + k_width :].astype(bf16)
    all_kv, wo_all, gu_all, wd_all = gather_both(
        ctx_count,
        jnp.concatenate([key_rows.reshape(row_count, k_width), value_rows], axis=1),
        [w_out, jnp.concatenate([w_gate, w_up], axis=1), w_down],
        1,
    )
    kv_seqs = all_kv.reshape(ctx_count, seq_count, pair_rows, 2 * k_width)
    kv_seqs = jnp.swapaxes(kv_seqs, 0, 1).reshape(seq_count, full_len, 2 * k_width)
    all_keys, all_values = kv_seqs[..., :k_width], kv_seqs[..., k_width:]
    query_seqs = query_rows.reshape(seq_count, pair_rows, HK, group_size, HD)

    def forward_group(parts):
        query_grp, key_grp, value_grp = parts
        scores = (
            jnp.einsum("qrd,kd->rqk", query_grp, key_grp, preferred_element_type=f32) * score_scale
        )
        scores = jnp.where(allowed, scores, -1e30)
        row_max = jnp.max(scores, axis=-1, keepdims=True)
        raised = jnp.exp(scores - row_max)
        row_sum = jnp.sum(raised, axis=-1, keepdims=True)
        probs = (raised / row_sum).astype(bf16)
        attended = jnp.einsum("rqk,kd->qrd", probs, value_grp, preferred_element_type=f32)
        return (attended.astype(bf16), (row_max + jnp.log(row_sum))[..., 0])

    def forward_seq(inputs):
        query_blk, key_blk, value_blk = inputs
        key_full = jnp.moveaxis(key_blk.reshape(full_len, HK, HD), 1, 0)
        value_full = jnp.moveaxis(value_blk.reshape(full_len, HK, HD), 1, 0)
        attended, log_sum = lax.map(
            forward_group, (jnp.moveaxis(query_blk, 1, 0), key_full, value_full)
        )
        return (jnp.moveaxis(attended, 0, 1).reshape(pair_rows, HQ * HD), log_sum)

    mixed_seqs, log_sums = lax.map(forward_seq, (query_seqs, all_keys, all_values))
    mixed_rows = mixed_seqs.reshape(row_count, HQ * HD)
    middle = x_rows + jnp.dot(mixed_rows, wo_all, preferred_element_type=f32)
    inverse_two = lax.rsqrt(jnp.mean(middle * middle, axis=-1, keepdims=True) + EPS)
    second_in = (middle * inverse_two * gain_second.astype(f32)).astype(bf16)
    gate_up = jnp.dot(second_in, gu_all, preferred_element_type=f32)
    hidden_width = gate_up.shape[1] // 2
    gate_proj, up_proj = gate_up[:, :hidden_width], gate_up[:, hidden_width:]
    hidden = (jax.nn.silu(gate_proj) * up_proj).astype(bf16)
    out_rows = middle + jnp.dot(hidden, wd_all, preferred_element_type=f32)
    result = out_rows.astype(bf16).reshape(hidden_in.shape)
    grad_rows = cotangent.reshape(row_count, width).astype(f32)
    grad_branch = grad_rows.astype(bf16)
    dw_down = jnp.einsum("rd,rf->df", grad_branch, hidden, preferred_element_type=f32)
    grad_hidden = jnp.einsum("rd,fd->rf", grad_branch, wd_all, preferred_element_type=f32)
    sigmoid_gate = jax.nn.sigmoid(gate_proj)
    grad_gate_proj = (
        grad_hidden * up_proj * sigmoid_gate * (1.0 + gate_proj * (1.0 - sigmoid_gate))
    ).astype(bf16)
    grad_up_proj = (grad_hidden * gate_proj * sigmoid_gate).astype(bf16)
    grad_gu = jnp.concatenate([grad_gate_proj, grad_up_proj], axis=1)
    dw_gu = jnp.einsum("rd,rf->df", second_in, grad_gu, preferred_element_type=f32)
    grad_second = jnp.einsum("rf,df->rd", grad_gu, gu_all, preferred_element_type=f32)
    grad_norm_two, dg_second = norm_back(
        middle, inverse_two, gain_second.astype(f32), grad_second
    )
    grad_middle = grad_rows + grad_norm_two
    grad_attn = grad_middle.astype(bf16)
    dw_out = jnp.einsum("rf,rd->fd", mixed_rows, grad_attn, preferred_element_type=f32)
    grad_mixed = jnp.einsum("rd,fd->rf", grad_attn, wo_all, preferred_element_type=f32).astype(
        bf16
    )
    grad_mixed_seqs = grad_mixed.reshape(seq_count, pair_rows, HK, group_size, HD)
    def backward_group(parts):
        query_grp, key_grp, value_grp, grad_grp, log_grp = parts
        scores = (
            jnp.einsum("qrd,kd->rqk", query_grp, key_grp, preferred_element_type=f32) * score_scale
        )
        scores = jnp.where(allowed, scores, -1e30)
        probs = jnp.exp(scores - log_grp[..., None])
        grad_probs = jnp.einsum("qrd,kd->rqk", grad_grp, value_grp, preferred_element_type=f32)
        row_dot = jnp.sum(grad_probs * probs, axis=-1, keepdims=True)
        grad_scores = (probs * (grad_probs - row_dot)).astype(bf16)
        grad_query_grp = (
            jnp.einsum("rqk,kd->qrd", grad_scores, key_grp, preferred_element_type=f32)
            * score_scale
        )
        grad_key_grp = (
            jnp.einsum("rqk,qrd->kd", grad_scores, query_grp, preferred_element_type=f32)
            * score_scale
        )
        grad_value_grp = jnp.einsum(
            "rqk,qrd->kd", probs.astype(bf16), grad_grp, preferred_element_type=f32
        )
        return (grad_query_grp, grad_key_grp, grad_value_grp)

    def backward_seq(inputs):
        query_blk, key_blk, value_blk, grad_blk, log_blk = inputs
        key_full = jnp.moveaxis(key_blk.reshape(full_len, HK, HD), 1, 0)
        value_full = jnp.moveaxis(value_blk.reshape(full_len, HK, HD), 1, 0)
        grad_query_all, grad_key_all, grad_value_all = lax.map(
            backward_group,
            (
                jnp.moveaxis(query_blk, 1, 0),
                key_full,
                value_full,
                jnp.moveaxis(grad_blk, 1, 0),
                log_blk,
            ),
        )
        return (
            jnp.moveaxis(grad_query_all, 0, 1).reshape(pair_rows, HQ * HD),
            jnp.moveaxis(grad_key_all, 0, 1).reshape(full_len, HK * HD),
            jnp.moveaxis(grad_value_all, 0, 1).reshape(full_len, HK * HD),
        )

    grad_query_seqs, grad_key_seqs, grad_value_seqs = lax.map(
        backward_seq, (query_seqs, all_keys, all_values, grad_mixed_seqs, log_sums)
    )
    dw_gu, dw_down, dw_out = (item.astype(bf16) for item in (dw_gu, dw_down, dw_out))
    piece = width // 4
    slab = dw_gu.shape[1] // 4
    down_cols = dw_down.shape[1] // 4
    pack_f = jnp.concatenate(
        [
            jnp.swapaxes(dw_gu.reshape(4, piece, 4, slab), 1, 2).reshape(4, 4 * piece, slab),
            dw_down.reshape(2, width // 2, 4, down_cols)
            .transpose(2, 1, 0, 3)
            .reshape(4, width // 2, slab),
            jnp.pad(dw_out.reshape(4, piece, width), ((0, 0), (0, 0), (0, slab - width))),
            jnp.pad(
                dg_second.astype(bf16).reshape(4, 1, piece), ((0, 0), (0, 0), (0, slab - piece))
            ),
        ],
        axis=1,
    )
    used_f = pack_f.shape[1]
    unit = 16 * ctx_count
    pack_f = jnp.pad(pack_f, ((0, 0), (0, -used_f % unit), (0, 0)))
    dkv = jnp.concatenate([grad_key_seqs, grad_value_seqs], axis=-1).astype(bf16)
    dkv = jnp.swapaxes(
        dkv.reshape(seq_count, ctx_count, pair_rows, 2 * k_width), 0, 1
    ).reshape(ctx_count, row_count, 2 * k_width)
    own_kv, part_f = kv_back(ctx_count, dkv, pack_f, 2)
    own_key_grad, own_value_grad = own_kv[:, :k_width], own_kv[:, k_width:]
    grad_query_lin = (
        rotate(grad_query_seqs.reshape(row_count, HQ, HD), cosine, -sine)
        .reshape(row_count, HQ * HD)
        .astype(bf16)
    )
    grad_key_lin = (
        rotate(own_key_grad.reshape(row_count, HK, HD), cosine, -sine)
        .reshape(row_count, HK * HD)
        .astype(bf16)
    )
    grad_value_lin = own_value_grad.reshape(row_count, HK * HD).astype(bf16)
    grad_lin = jnp.concatenate([grad_query_lin, grad_key_lin, grad_value_lin], axis=1)
    dw_qkv = jnp.einsum("rd,rf->df", first_in, grad_lin, preferred_element_type=f32)
    grad_first = jnp.einsum("rf,df->rd", grad_lin, qkv_all, preferred_element_type=f32)
    grad_norm_one, dg_first = norm_back(x_rows, inverse_one, gain_first.astype(f32), grad_first)
    grad_in_rows = grad_middle + grad_norm_one
    narrow = 256
    pack_q = jnp.pad(dw_qkv.astype(bf16), ((0, 0), (0, -dw_qkv.shape[1] % narrow)))
    strips = pack_q.shape[1] // narrow
    pack_q = jnp.swapaxes(pack_q.reshape(4, piece, strips, narrow), 1, 2)
    pack_q = jnp.concatenate(
        [
            pack_q.reshape(4, strips * piece, narrow),
            jnp.pad(
                dg_first.astype(bf16).reshape(4, 1, piece), ((0, 0), (0, 0), (0, narrow - piece))
            ),
        ],
        axis=1,
    )
    pack_q = jnp.pad(pack_q, ((0, 0), (0, -pack_q.shape[1] % unit), (0, 0)))
    total_f, total_q = last_sum(ctx_count, part_f, pack_q, 3)
    total_f, total_q = total_f.astype(f32), total_q.astype(f32)
    out_gu = jnp.swapaxes(total_f[: 4 * piece].reshape(4, piece, slab), 0, 1).reshape(piece, -1)
    at = 4 * piece
    out_down = total_f[at : at + width // 2].reshape(width // 2, 2, down_cols)
    out_down = jnp.swapaxes(out_down, 0, 1).reshape(width, down_cols).T
    at += width // 2
    out_wo = total_f[at : at + piece, :width]
    out_g2 = total_f[at + piece, :piece]
    at = strips * piece
    out_qkv = jnp.swapaxes(total_q[:at].reshape(strips, piece, narrow), 0, 1).reshape(piece, -1)
    return (
        result,
        grad_in_rows.reshape(hidden_in.shape),
        out_qkv[:, :q_width],
        out_qkv[:, q_width : q_width + k_width],
        out_qkv[:, q_width + k_width : q_width + 2 * k_width],
        out_wo,
        out_gu[:, :hidden_width],
        out_gu[:, hidden_width:],
        out_down,
        total_q[at, :piece],
        out_g2,
    )


def solution(mesh):
    in_specs = (
        P("fsdp", "ctx", None, None),
        P("fsdp", "ctx", None, None),
        P(),
        P("fsdp", "ctx", None),
        P("fsdp"),
        P("fsdp", None),
        P("fsdp", None),
        P("fsdp", None),
        P("fsdp", None),
        P("fsdp"),
        P("fsdp", None),
        P("fsdp", None),
        P("fsdp", None),
    )
    out_specs = (
        P("fsdp", "ctx", None, None),
        P("fsdp", "ctx", None, None),
        P("fsdp", None),
        P("fsdp", None),
        P("fsdp", None),
        P("fsdp", None),
        P("fsdp", None),
        P("fsdp", None),
        P("fsdp", None),
        P("fsdp"),
        P("fsdp"),
    )
    return jax.shard_map(shards, mesh=mesh, in_specs=in_specs, out_specs=out_specs, check_vma=False)
```

time: 800 us -> 460 us (0.57)
  waiting for transfers between devices: 348 us -> 0 us
  blocking collectives: 193 us -> 0 us
  Pallas kernels: 0 us -> 156 us
  local copies, waits for them, and re-layouts: 90.6 us -> 151 us
  matrix products: 116 us -> 101 us
  other arithmetic: 25.4 us -> 40.3 us
  between operations: 16.4 us -> 1.6 us
    reduce_scatter x8 -> x0, waiting for transfers between devices: 245 us -> none  [the longest x1 78.9 us: shards(): lax.psum_scatter(grad_value_seqs, 'ctx', scatter_dimension=1, tiled=True)]
    pallas_call x0 -> x4, Pallas kernels: none -> 156 us  [comm_call(): pl.pallas_call(kernel, out_shape=out_shape, in_specs=[vm] * len(args), ou...]
    psum x1 -> x0, blocking collectives: 149 us -> none  [shards(): lax.psum((shares[0], shares[1], shares[2], shares[3], shares[4], shares[5...]
    all_gather x5 -> x0, waiting for transfers between devices: 70.7 us -> none  [the longest x1 46.1 us: shards(): lax.all_gather(outgoing[1], 'ctx', axis=1, tiled=True)]
    reshape x2 -> x11, local copies, waits for them, and re-layouts: 1.01 us -> 33.5 us  [the longest x2 12 us: shards(): dw_gu.reshape(4, piece, 4, slab)]
    unnamed x15 -> x0, waiting for transfers between devices: 32.4 us -> none
    all_gather x4 -> x0, blocking collectives: 29.4 us -> none  [the longest x1 8.89 us: shards(): lax.all_gather(w_out, 'fsdp', axis=0, tiled=True)]
    dot_general x18 -> x9, matrix products: 41.3 us -> 22.9 us  [the longest x1 3.83 us: shards(): jnp.einsum('rd,rf->df', second_in, grad_gu, preferred_element_type=f32)]
  transfers between devices with their start and end apart: 14 -> 0, of which waited for: 10 -> 0; matrix products, arithmetic and copies ran while one was open for 24% -> 0% of each run, Pallas kernels for 0% -> 0%
where the time goes in v1:
time: 460 us; the launch traced here: 451 us
  Pallas kernels  156 us (34%)
  local copies, waits for them, and re-layouts  151 us (33%)
  matrix products  101 us (22%)
  other arithmetic  40.3 us (9%)
    pallas_call x4, Pallas kernels, comm_call(): pl.pallas_call(kernel, out_shape=out_shape, in_specs=[vm] * len(args), ou...  156 us
    dynamic_update_slice x6, local copies, waits for them, and re-layouts, shards(): lax.map(backward_seq, (query_seqs, all_keys, all_values, grad_mixed_seqs,...  34.4 us
    dot_general x6, matrix products, forward_group(): jnp.einsum('rqk,kd->qrd', probs, value_grp, preferred_element_type=f32)  21.2 us
    unnamed x95, local copies, waits for them, and re-layouts  14.4 us
    dot_general x6, matrix products, forward_group(): jnp.einsum('qrd,kd->rqk', query_grp, key_grp, preferred_element_type=f32)  12.9 us
    dot_general x6, matrix products, backward_group(): jnp.einsum('qrd,kd->rqk', query_grp, key_grp, preferred_element_type=f32)  12.1 us
    reshape x2, local copies, waits for them, and re-layouts, shards(): dw_gu.reshape(4, piece, 4, slab)  12 us

profile of v1, /device:TPU:0, one launch (start us, length us, event | category | flops | bytes accessed | tf_op | source)
XLA Modules:
  0.0 450.6 jit_solution(5651549777485724095)
XLA Ops:
  12.6 14.0 %shard_map.212 = (bf16[576,960]{1,0:T(8,128)(2,1)}, bf16[64,144]{1,0:T(8,128)(2,1)}) custom-call(bf16[144,960]{1,0:T(8,128)(2,1)} %pad_maximum_fusion.11.refs_0_, bf16[16,144]{1,0:T(8,128)(2,1)} %maximum_maximum_fusion.refs_1_), custom_call_target="tpu_custom_call" | custom-call | tf_op jit(solution)/shard_map/pallas_call | solution.py:92
  36.7 43.9 %shard_map.213 = (bf16[8,512,384]{2,1,0:T(8,128)(2,1)}, bf16[576,576]{1,0:T(8,128)(2,1)}, bf16[576,3072]{1,0:T(8,128)(2,1)}, bf16[1536,576]{1,0:T(8,128)(2,1)}) custom-call(bf16[512,384]{1,0:T(8,128)(2,1)} %pad_maximum_fusion.10.kv_ref, bf16[144,576]{1,0:T(8,128)(2,1)} %refs_0_.1, bf16[144,3072]{1,0:T(8,128)(2,1)} %pad_maximum_fusion.5.refs_1_, ...), custom_call_target="tpu_custom_call" | custom-call | tf_op jit(solution)/shard_map/pallas_call | solution.py:92
  80.6 5.3 %copy.90 = bf16[2,8,256,384]{2,1,3,0:T(8,128)(2,1)} copy(bf16[2,8,256,384]{3,2,0,1:T(8,128)(2,1)} %bitcast.360) | data formatting | bytes 6291456 | tf_op jit(solution)/shard_map/transpose | solution.py:605
  85.9 5.9 %reshape.445 = bf16[2,2048,384]{1,2,0:T(8,128)(2,1)} reshape(bf16[2,8,256,384]{2,1,3,0:T(8,128)(2,1)} %copy.90) | data formatting | bytes 6291456 | tf_op jit(solution)/shard_map/reshape | solution.py:605
  95.2 53.8 %while.57 = (s32[]{:T(128)}, bf16[2,256,576]{1,2,0:T(8,128)(2,1)}, f32[2,3,3,256]{3,2,1,0:T(4,128)}, bf16[2,256,3,3,64]{1,4,3,2,0:T(8,128)(2,1)S(1)}, bf16[2,204...) while((s32[]{:T(128)}, bf16[2,256,576]{1,2,0:T(8,128)(2,1)}, ...), condition=%wide.region_6.7_spmd.clone, body=%wide.region_1.6_spmd.clone.sunk | while | flops 422100224 | bytes 26078508 | solution.py:631
  98.5 21.3 %while.60 = (s32[]{:T(128)}, bf16[3,256,3,64]{1,3,2,0:T(8,128)(2,1)}, f32[3,3,256]{2,1,0:T(4,128)S(1)}, bf16[3,2048,64]{1,2,0:T(8,128)(2,1)}, pred[1,256,2048]{1...) while((s32[]{:T(128)}, ...), condition=%wide.region_5.5_spmd, body=%wide.region_2.4_spmd.sunk | while | flops 421575936 | bytes 21197920 | solution.py:626
  102.0 3.5 fusion.135
  125.4 21.3 %while.60 = (s32[]{:T(128)}, bf16[3,256,3,64]{1,3,2,0:T(8,128)(2,1)}, f32[3,3,256]{2,1,0:T(4,128)S(1)}, bf16[3,2048,64]{1,2,0:T(8,128)(2,1)}, pred[1,256,2048]{1...) while((s32[]{:T(128)}, ...), condition=%wide.region_5.5_spmd, body=%wide.region_2.4_spmd.sunk | while | flops 421575936 | bytes 21197920 | solution.py:626
  171.9 3.8 convolution_convert_fusion
  179.8 4.1 reshape.454
  183.9 4.6 %copy.136 = bf16[2,288,4,384]{3,0,1,2:T(2,128)(2,1)} copy(bf16[2,288,4,384]{3,2,1,0:T(4,128)(2,1)} %reshape.454) | data formatting | bytes 3538944 | tf_op jit(solution)/shard_map/reshape | solution.py:717
  188.4 5.2 %reshape.455 = bf16[4,288,768]{2,1,0:T(8,128)(2,1)} reshape(bf16[4,288,2,384]{3,2,1,0:T(2,128)(2,1)} %bitcast.350) | data formatting | bytes 3538944 | tf_op jit(solution)/shard_map/reshape | solution.py:719
  193.6 7.8 %reshape.452 = bf16[4,144,4,768]{3,2,1,0:T(4,128)(2,1)} reshape(bf16[576,3072]{1,0:T(8,128)(2,1)} %convolution_convert_fusion) | data formatting | bytes 7077888 | tf_op jit(solution)/shard_map/reshape | solution.py:716
  201.4 4.2 copy.100
  205.6 93.7 %while.59 = (s32[]{:T(128)}, f32[2,256,576]{1,0,2:T(2,128)}, bf16[2,2048,192]{1,2,0:T(8,128)(2,1)}, bf16[2,2048,192]{1,2,0:T(8,128)(2,1)}, bf16[2,256,3,3,64]{1,...) while((s32[]{:T(128)}, f32[2,256,576]{1,0,2:T(2,128)}, ...), condition=%wide.region_13.14_spmd.clone, body=%wide.region_9.13_spmd.clone.sunk | while | flops 1021492480 | bytes 96780992 | solution.py:707
  209.4 25.8 %while.61 = (s32[]{:T(128)}, f32[3,256,3,64]{1,3,2,0:T(8,128)}, bf16[3,2048,64]{1,2,0:T(8,128)(2,1)}, bf16[3,2048,64]{1,2,0:T(8,128)(2,1)S(1)}, bf16[3,2048,64]{...) while((s32[]{:T(128)}, f32[3,256,3,64]{1,3,2,0:T(8,128)}, ...), condition=%wide.region_12.12_spmd, body=%wide.region_10.11_spmd.sunk | while | flops 1020968192 | bytes 56448176 | solution.py:691
  237.2 12.7 %dynamic_update_slice.64 = f32[2,256,576]{1,0,2:T(2,128)} dynamic-update-slice(f32[2,256,576]{1,0,2:T(2,128)} %get-tuple-element.854, f32[1,256,576]{1,0,2:T(1,128)S(1)} %copy.138, s32[]{:T(128)S(6)} %copy.183, s32[]{:T(128)} %constant.125.clone.1..sunk.1, s32[]{:T(128)} %constant.125.clone.1..sunk.1) | dynamic-update-slice | bytes 1179652 | tf_op jit(solution)/shard_map/while/body/jit(dynamic_update_index_in_dim)/dynamic_update_slice | solution.py:707
  256.2 25.8 %while.61 = (s32[]{:T(128)}, f32[3,256,3,64]{1,3,2,0:T(8,128)}, bf16[3,2048,64]{1,2,0:T(8,128)(2,1)}, bf16[3,2048,64]{1,2,0:T(8,128)(2,1)S(1)}, bf16[3,2048,64]{...) while((s32[]{:T(128)}, f32[3,256,3,64]{1,3,2,0:T(8,128)}, ...), condition=%wide.region_12.12_spmd, body=%wide.region_10.11_spmd.sunk | while | flops 1020968192 | bytes 56448176 | solution.py:691
  284.0 12.7 %dynamic_update_slice.64 = f32[2,256,576]{1,0,2:T(2,128)} dynamic-update-slice(f32[2,256,576]{1,0,2:T(2,128)} %get-tuple-element.854, f32[1,256,576]{1,0,2:T(1,128)S(1)} %copy.138, s32[]{:T(128)S(6)} %copy.183, s32[]{:T(128)} %constant.125.clone.1..sunk.1, s32[]{:T(128)} %constant.125.clone.1..sunk.1) | dynamic-update-slice | bytes 1179652 | tf_op jit(solution)/shard_map/while/body/jit(dynamic_update_index_in_dim)/dynamic_update_slice | solution.py:707
  309.0 4.1 copy.99
  318.8 4.4 copy.98
  323.2 5.1 %pad_maximum_fusion.1 = bf16[2,8,256,384]{3,2,0,1:T(8,128)(2,1)} fusion(bf16[2,8,256,192]{3,2,0,1:T(8,128)(2,1)} %copy.99, bf16[2,8,256,192]{3,2,0,1:T(8,128)(2,1)} %copy.98), kind=kLoop, calls=%fused_computation.88 | loop fusion | flops 6291456 | bytes 6291456 | tf_op jit(solution)/shard_map/concatenate | solution.py:730
  328.3 45.7 %shard_map.214 = (f32[512,384]{1,0:T(8,128)}, bf16[1024,768]{1,0:T(8,128)(2,1)}) custom-call(bf16[8,512,384]{2,1,0:T(8,128)(2,1)} %bitcast.346, bf16[4,1024,768]{2,1,0:T(8,128)(2,1)} %pad.26.pack), custom_call_target="tpu_custom_call" | custom-call | tf_op jit(solution)/shard_map/pallas_call | solution.py:92
  388.9 52.3 %shard_map.215 = (bf16[1024,768]{1,0:T(8,128)(2,1)}, bf16[640,256]{1,0:T(8,128)(2,1)}) custom-call(bf16[1024,768]{1,0:T(8,128)(2,1)} %get-tuple-element.217.part, bf16[4,640,256]{2,1,0:T(8,128)(2,1)} %pad.29.pack), custom_call_target="tpu_custom_call" | custom-call | tf_op jit(solution)/shard_map/pallas_call | solution.py:92
  (346 shorter events, 209.1 us)
Async XLA Ops:
  0.6 8.4 %copy-start.34 = (bf16[384,576]{0,1:T(8,128)(2,1)S(1)}, bf16[384,576]{0,1:T(8,128)(2,1)}, u32[]{:S(2)}) copy-start(bf16[384,576]{0,1:T(8,128)(2,1)} %param.33) | copy-start | bytes 1327108
  0.7 9.4 %copy-start.29 = (bf16[2,1,256,576]{2,3,1,0:T(8,128)(2,1)S(1)}, bf16[2,1,256,576]{2,3,1,0:T(8,128)(2,1)}, u32[]{:S(2)}) copy-start(bf16[2,1,256,576]{2,3,1,0:T(8,128)(2,1)} %param.22) | copy-start | bytes 1769476
  4.7 24.2 %copy-start.42 = (f32[1,2,2,128]{3,1,2,0:T(2,128)}, f32[1,2,2,128]{3,1,2,0:T(2,128)S(1)}, u32[]{:S(2)}) copy-start(f32[1,2,2,128]{3,1,2,0:T(2,128)S(1)} %copy.130) | copy-start | bytes 6148
  7.2 26.7 %copy-start.24 = (f32[512,32]{0,1:T(8,128)}, f32[512,32]{0,1:T(8,128)S(1)}, u32[]{:S(2)}) copy-start(f32[512,32]{0,1:T(8,128)S(1)} %get-tuple-element.458) | copy-start | bytes 196612
  10.6 17.6 %copy-start.23 = (bf16[2,1,256,576]{2,3,1,0:T(8,128)(2,1)S(1)}, bf16[2,1,256,576]{2,3,1,0:T(8,128)(2,1)}, u32[]{:S(2)}) copy-start(bf16[2,1,256,576]{2,3,1,0:T(8,128)(2,1)} %param.21) | copy-start | bytes 1769476
  28.9 2.7 copy-start.9
  152.6 2.8 copy-start.21
  152.7 2.8 copy-start.45
  171.9 6.2 %copy-start.12 = (f32[512,576]{0,1:T(8,128)}, f32[512,576]{0,1:T(8,128)S(1)}, u32[]{:S(2)}) copy-start(f32[512,576]{0,1:T(8,128)S(1)} %subtract_add_fusion.1) | copy-start | bytes 3538948
  171.9 3.8 copy-start.22
  171.9 3.8 copy-start.47
  235.2 14.7 %copy-start.8 = (bf16[3,2048,64]{1,2,0:T(8,128)(2,1)S(1)}, bf16[3,2048,64]{1,2,0:T(8,128)(2,1)}, u32[]{:S(2)}) copy-start(bf16[3,2048,64]{1,2,0:T(8,128)(2,1)} %get-tuple-element.723) | copy-start | bytes 2359300 | tf_op jit(solution)/shard_map/while
  282.0 14.7 %copy-start.8 = (bf16[3,2048,64]{1,2,0:T(8,128)(2,1)S(1)}, bf16[3,2048,64]{1,2,0:T(8,128)(2,1)}, u32[]{:S(2)}) copy-start(bf16[3,2048,64]{1,2,0:T(8,128)(2,1)} %get-tuple-element.723) | copy-start | bytes 2359300 | tf_op jit(solution)/shard_map/while
  296.7 2.6 copy-start.1
  296.7 2.6 copy-start.4
  296.7 2.6 copy-start.28
  299.3 3.3 copy-start.13
  299.3 3.3 copy-start.18
  299.4 4.0 copy-start.14
  375.9 2.6 copy-start.41
  375.9 2.6 copy-start.43
  378.4 3.5 copy-start.35
  378.5 3.4 copy-start.37
  443.7 2.7 copy-start.16
  (48 other events, 85.8 us)

commit v2 on v1

--- a/solution.py
+++ b/solution.py
@@ -540,6 +540,155 @@
     )
 
 
+def dot_t(left, right):
+    return lax.dot_general(left, right, (((1,), (1,)), ((), ())), preferred_element_type=jnp.float32)
+
+
+def head_stack(ref, rows, group, size):
+    return jnp.concatenate(
+        [ref[rows, (group * size + j) * HD : (group * size + j + 1) * HD] for j in range(size)],
+        axis=0,
+    )
+
+
+def key_block(kv_ref, rows, first):
+    block = kv_ref[:, rows, first : first + HD]
+    return block.reshape(block.shape[0] * block.shape[1], HD)
+
+
+def with_bias(scores, bias, size):
+    span = bias.shape[0]
+    return (scores.reshape(size, span, -1) + bias[None]).reshape(scores.shape)
+
+
+def attend_kernel(pair, q_ref, kv_ref, bias_ref, o_ref, lse_ref):
+    size = HQ // HK
+    span = pair // 2
+    f32 = jnp.float32
+    bf16 = jnp.bfloat16
+
+    def sequence(s, carry):
+        low = pl.ds(pl.multiple_of(s * pair, 16), span)
+        high = pl.ds(pl.multiple_of(s * pair + span, 16), span)
+        for g in range(HK):
+            keys = [key_block(kv_ref, rows, g * HD) for rows in (low, high)]
+            values = [key_block(kv_ref, rows, (HK + g) * HD) for rows in (low, high)]
+            for part, rows in enumerate((low, high)):
+                query = head_stack(q_ref, rows, g, size)
+                blocks = [dot_t(query, keys[j]) for j in range(part + 1)]
+                blocks[part] = with_bias(blocks[part], bias_ref[part], size)
+                top = jnp.max(blocks[0], axis=-1, keepdims=True)
+                if part:
+                    top = jnp.maximum(top, jnp.max(blocks[1], axis=-1, keepdims=True))
+                total, out = 0.0, 0.0
+                for j, block in enumerate(blocks):
+                    raised = jnp.exp(block - top)
+                    total = total + jnp.sum(raised, axis=-1, keepdims=True)
+                    out = out + jnp.dot(
+                        raised.astype(bf16), values[j], preferred_element_type=f32
+                    )
+                out = (out / total).astype(bf16)
+                lse = top + jnp.log(total)
+                for j in range(size):
+                    h = g * size + j
+                    o_ref[rows, h * HD : (h + 1) * HD] = out[j * span : (j + 1) * span]
+                    lse_ref[rows, h : h + 1] = lse[j * span : (j + 1) * span]
+        return carry
+
+    lax.fori_loop(0, q_ref.shape[0] // pair, sequence, 0)
+
+
+def attend_back_kernel(pair, q_ref, kv_ref, bias_ref, o_ref, do_ref, lse_ref, dq_ref, dkv_ref):
+    size = HQ // HK
+    span = pair // 2
+    count = kv_ref.shape[0]
+    f32 = jnp.float32
+    bf16 = jnp.bfloat16
+    scale = 1.0 / math.sqrt(HD)
+
+    def sequence(s, carry):
+        low = pl.ds(pl.multiple_of(s * pair, 16), span)
+        high = pl.ds(pl.multiple_of(s * pair + span, 16), span)
+        for g in range(HK):
+            keys = [key_block(kv_ref, rows, g * HD) for rows in (low, high)]
+            values = [key_block(kv_ref, rows, (HK + g) * HD) for rows in (low, high)]
+            key_grads, value_grads = [0.0, 0.0], [0.0, 0.0]
+            for part, rows in enumerate((low, high)):
+                query = head_stack(q_ref, rows, g, size)
+                grad = head_stack(do_ref, rows, g, size)
+                out = head_stack(o_ref, rows, g, size)
+                lse = jnp.concatenate(
+                    [lse_ref[rows, g * size + j : g * size + j + 1] for j in range(size)], axis=0
+                )
+                inner = jnp.sum(grad.astype(f32) * out.astype(f32), axis=-1, keepdims=True)
+                query_t = query.astype(f32).T.astype(bf16)
+                grad_t = grad.astype(f32).T.astype(bf16)
+                dq = 0.0
+                for j in range(part + 1):
+                    scores = dot_t(query, keys[j])
+                    if j == part:
+                        scores = with_bias(scores, bias_ref[part], size)
+                    probs = jnp.exp(scores - lse)
+                    ds = (probs * (dot_t(grad, values[j]) - inner)).astype(bf16)
+                    dq = dq + jnp.dot(ds, keys[j], preferred_element_type=f32)
+                    key_grads[j] = key_grads[j] + jnp.dot(query_t, ds, preferred_element_type=f32)
+                    value_grads[j] = value_grads[j] + jnp.dot(
+                        grad_t, probs.astype(bf16), preferred_element_type=f32
+                    )
+                dq = dq * scale
+                for j in range(size):
+                    h = g * size + j
+                    dq_ref[rows, h * HD : (h + 1) * HD] = dq[j * span : (j + 1) * span]
+            for j, rows in enumerate((low, high)):
+                for first, item in ((g * HD, key_grads[j]), ((HK + g) * HD, value_grads[j])):
+                    dkv_ref[:, rows, first : first + HD] = (
+                        item.T.astype(bf16).reshape(count, span, HD)
+                    )
+        return carry
+
+    lax.fori_loop(0, q_ref.shape[0] // pair, sequence, 0)
+
+
+def plain_call(kernel, out_shape, args, flops):
+    vm = pl.BlockSpec(memory_space=VMEM)
+    return pl.pallas_call(
+        kernel,
+        out_shape=out_shape,
+        in_specs=[vm] * len(args),
+        out_specs=jax.tree.map(lambda _: vm, out_shape),
+        compiler_params=pltpu.CompilerParams(vmem_limit_bytes=BIG),
+        cost_estimate=pl.CostEstimate(flops=flops, bytes_accessed=8_000_000, transcendentals=0),
+    )(*args)
+
+
+def pack_kernel(second_t, gu_ref, branch_t, hidden_ref, mixed_t, ga_ref, gain_ref, out_ref):
+    f32 = jnp.float32
+    bf16 = jnp.bfloat16
+    width = second_t.shape[0]
+    piece = width // 4
+    slab = out_ref.shape[2]
+    cols = hidden_ref.shape[1] // 4
+    deep = width // 2
+    at = 4 * piece + deep
+    for f in range(4):
+        mine = pl.ds(f * piece, piece)
+        for s in range(4):
+            out_ref[f, s * piece : (s + 1) * piece] = jnp.dot(
+                second_t[mine], gu_ref[:, s * slab : (s + 1) * slab], preferred_element_type=f32
+            ).astype(bf16)
+        for h in range(2):
+            out_ref[f, 4 * piece : at, h * cols : (h + 1) * cols] = jnp.dot(
+                branch_t[h * deep : (h + 1) * deep],
+                hidden_ref[:, f * cols : (f + 1) * cols],
+                preferred_element_type=f32,
+            ).astype(bf16)
+        out_ref[f, at : at + piece, :width] = jnp.dot(
+            mixed_t[mine], ga_ref[...], preferred_element_type=f32
+        ).astype(bf16)
+        out_ref[f, at : at + piece, width:] = jnp.zeros((piece, slab - width), bf16)
+        out_ref[f, at + piece :] = gain_ref[f]
+
+
 def shards(
     hidden_in,
     cotangent,
@@ -562,17 +711,20 @@
     ctx_count = lax.axis_size("ctx")
     full_len = ctx_count * pair_rows
     row_count = seq_count * pair_rows
-    group_size = HQ // HK
     score_scale = 1.0 / math.sqrt(HD)
     f32 = jnp.float32
     bf16 = jnp.bfloat16
-    columns = jnp.arange(pair_rows, dtype=jnp.int32)
-    span_ids = jnp.where(
-        columns[None, :] < span_rows, span_table[:, None], 2 * ctx_count - 1 - span_table[:, None]
-    )
-    key_order = (span_ids * span_rows + columns[None, :] % span_rows).reshape(full_len)
-    own_order = lax.dynamic_slice_in_dim(key_order, lax.axis_index("ctx") * pair_rows, pair_rows)
-    allowed = (key_order[None, :] <= own_order[:, None])[None, :, :]
+    places = jnp.arange(span_rows, dtype=jnp.int32)
+    own_span = span_table[lax.axis_index("ctx")]
+    bias = []
+    for ids, own in (
+        (span_table, own_span),
+        (2 * ctx_count - 1 - span_table, 2 * ctx_count - 1 - own_span),
+    ):
+        key_order = (ids[:, None] * span_rows + places[None, :]).reshape(-1)
+        query_order = own * span_rows + places
+        bias.append(jnp.where(key_order[None, :] <= query_order[:, None], 0.0, -1e30))
+    bias = jnp.stack(bias).astype(f32)
     gains_own = jnp.concatenate(
         [attn_gain[None], ffn_gain[None], jnp.zeros((14,) + attn_gain.shape, bf16)], axis=0
     )
@@ -601,35 +753,17 @@
         [w_out, jnp.concatenate([w_gate, w_up], axis=1), w_down],
         1,
     )
-    kv_seqs = all_kv.reshape(ctx_count, seq_count, pair_rows, 2 * k_width)
-    kv_seqs = jnp.swapaxes(kv_seqs, 0, 1).reshape(seq_count, full_len, 2 * k_width)
-    all_keys, all_values = kv_seqs[..., :k_width], kv_seqs[..., k_width:]
-    query_seqs = query_rows.reshape(seq_count, pair_rows, HK, group_size, HD)
-
-    def forward_group(parts):
-        query_grp, key_grp, value_grp = parts
-        scores = (
-            jnp.einsum("qrd,kd->rqk", query_grp, key_grp, preferred_element_type=f32) * score_scale
-        )
-        scores = jnp.where(allowed, scores, -1e30)
-        row_max = jnp.max(scores, axis=-1, keepdims=True)
-        raised = jnp.exp(scores - row_max)
-        row_sum = jnp.sum(raised, axis=-1, keepdims=True)
-        probs = (raised / row_sum).astype(bf16)
-        attended = jnp.einsum("rqk,kd->qrd", probs, value_grp, preferred_element_type=f32)
-        return (attended.astype(bf16), (row_max + jnp.log(row_sum))[..., 0])
-
-    def forward_seq(inputs):
-        query_blk, key_blk, value_blk = inputs
-        key_full = jnp.moveaxis(key_blk.reshape(full_len, HK, HD), 1, 0)
-        value_full = jnp.moveaxis(value_blk.reshape(full_len, HK, HD), 1, 0)
-        attended, log_sum = lax.map(
-            forward_group, (jnp.moveaxis(query_blk, 1, 0), key_full, value_full)
-        )
-        return (jnp.moveaxis(attended, 0, 1).reshape(pair_rows, HQ * HD), log_sum)
-
-    mixed_seqs, log_sums = lax.map(forward_seq, (query_seqs, all_keys, all_values))
-    mixed_rows = mixed_seqs.reshape(row_count, HQ * HD)
+    query_rows = query_rows.reshape(row_count, q_width) * jnp.asarray(score_scale, bf16)
+    flops = 4 * HQ * row_count * full_len * HD
+    mixed_rows, log_sums = plain_call(
+        functools.partial(attend_kernel, pair_rows),
+        [
+            jax.ShapeDtypeStruct((row_count, q_width), bf16),
+            jax.ShapeDtypeStruct((row_count, 128), f32),
+        ],
+        [query_rows, all_kv, bias],
+        flops,
+    )
     middle = x_rows + jnp.dot(mixed_rows, wo_all, preferred_element_type=f32)
     inverse_two = lax.rsqrt(jnp.mean(middle * middle, axis=-1, keepdims=True) + EPS)
     second_in = (middle * inverse_two * gain_second.astype(f32)).astype(bf16)
@@ -641,7 +775,6 @@
     result = out_rows.astype(bf16).reshape(hidden_in.shape)
     grad_rows = cotangent.reshape(row_count, width).astype(f32)
     grad_branch = grad_rows.astype(bf16)
-    dw_down = jnp.einsum("rd,rf->df", grad_branch, hidden, preferred_element_type=f32)
     grad_hidden = jnp.einsum("rd,fd->rf", grad_branch, wd_all, preferred_element_type=f32)
     sigmoid_gate = jax.nn.sigmoid(gate_proj)
     grad_gate_proj = (
@@ -649,92 +782,44 @@
     ).astype(bf16)
     grad_up_proj = (grad_hidden * gate_proj * sigmoid_gate).astype(bf16)
     grad_gu = jnp.concatenate([grad_gate_proj, grad_up_proj], axis=1)
-    dw_gu = jnp.einsum("rd,rf->df", second_in, grad_gu, preferred_element_type=f32)
     grad_second = jnp.einsum("rf,df->rd", grad_gu, gu_all, preferred_element_type=f32)
     grad_norm_two, dg_second = norm_back(
         middle, inverse_two, gain_second.astype(f32), grad_second
     )
     grad_middle = grad_rows + grad_norm_two
     grad_attn = grad_middle.astype(bf16)
-    dw_out = jnp.einsum("rf,rd->fd", mixed_rows, grad_attn, preferred_element_type=f32)
     grad_mixed = jnp.einsum("rd,fd->rf", grad_attn, wo_all, preferred_element_type=f32).astype(
         bf16
     )
-    grad_mixed_seqs = grad_mixed.reshape(seq_count, pair_rows, HK, group_size, HD)
-    def backward_group(parts):
-        query_grp, key_grp, value_grp, grad_grp, log_grp = parts
-        scores = (
-            jnp.einsum("qrd,kd->rqk", query_grp, key_grp, preferred_element_type=f32) * score_scale
-        )
-        scores = jnp.where(allowed, scores, -1e30)
-        probs = jnp.exp(scores - log_grp[..., None])
-        grad_probs = jnp.einsum("qrd,kd->rqk", grad_grp, value_grp, preferred_element_type=f32)
-        row_dot = jnp.sum(grad_probs * probs, axis=-1, keepdims=True)
-        grad_scores = (probs * (grad_probs - row_dot)).astype(bf16)
-        grad_query_grp = (
-            jnp.einsum("rqk,kd->qrd", grad_scores, key_grp, preferred_element_type=f32)
-            * score_scale
-        )
-        grad_key_grp = (
-            jnp.einsum("rqk,qrd->kd", grad_scores, query_grp, preferred_element_type=f32)
-            * score_scale
-        )
-        grad_value_grp = jnp.einsum(
-            "rqk,qrd->kd", probs.astype(bf16), grad_grp, preferred_element_type=f32
-        )
-        return (grad_query_grp, grad_key_grp, grad_value_grp)
-
-    def backward_seq(inputs):
-        query_blk, key_blk, value_blk, grad_blk, log_blk = inputs
-        key_full = jnp.moveaxis(key_blk.reshape(full_len, HK, HD), 1, 0)
-        value_full = jnp.moveaxis(value_blk.reshape(full_len, HK, HD), 1, 0)
-        grad_query_all, grad_key_all, grad_value_all = lax.map(
-            backward_group,
-            (
-                jnp.moveaxis(query_blk, 1, 0),
-                key_full,
-                value_full,
-                jnp.moveaxis(grad_blk, 1, 0),
-                log_blk,
-            ),
-        )
-        return (
-            jnp.moveaxis(grad_query_all, 0, 1).reshape(pair_rows, HQ * HD),
-            jnp.moveaxis(grad_key_all, 0, 1).reshape(full_len, HK * HD),
-            jnp.moveaxis(grad_value_all, 0, 1).reshape(full_len, HK * HD),
-        )
-
-    grad_query_seqs, grad_key_seqs, grad_value_seqs = lax.map(
-        backward_seq, (query_seqs, all_keys, all_values, grad_mixed_seqs, log_sums)
-    )
-    dw_gu, dw_down, dw_out = (item.astype(bf16) for item in (dw_gu, dw_down, dw_out))
     piece = width // 4
-    slab = dw_gu.shape[1] // 4
-    down_cols = dw_down.shape[1] // 4
-    pack_f = jnp.concatenate(
+    slab = grad_gu.shape[1] // 4
+    down_cols = hidden_width // 4
+    unit = 16 * ctx_count
+    used_f = 5 * piece + width // 2
+    rows_f = -(-(used_f + 1) // unit) * unit
+    gain_rows = jnp.pad(
+        dg_second.astype(bf16).reshape(4, 1, piece),
+        ((0, 0), (0, rows_f - used_f - 1), (0, slab - piece)),
+    )
+    pack_f = plain_call(
+        pack_kernel,
+        jax.ShapeDtypeStruct((4, rows_f, slab), bf16),
+        [second_in.T, grad_gu, grad_branch.T, hidden, mixed_rows.T, grad_attn, gain_rows],
+        3 * flops,
+    )
+    grad_query_rows, dkv = plain_call(
+        functools.partial(attend_back_kernel, pair_rows),
         [
-            jnp.swapaxes(dw_gu.reshape(4, piece, 4, slab), 1, 2).reshape(4, 4 * piece, slab),
-            dw_down.reshape(2, width // 2, 4, down_cols)
-            .transpose(2, 1, 0, 3)
-            .reshape(4, width // 2, slab),
-            jnp.pad(dw_out.reshape(4, piece, width), ((0, 0), (0, 0), (0, slab - width))),
-            jnp.pad(
-                dg_second.astype(bf16).reshape(4, 1, piece), ((0, 0), (0, 0), (0, slab - piece))
-            ),
+            jax.ShapeDtypeStruct((row_count, q_width), f32),
+            jax.ShapeDtypeStruct((ctx_count, row_count, 2 * k_width), bf16),
         ],
-        axis=1,
-    )
-    used_f = pack_f.shape[1]
-    unit = 16 * ctx_count
-    pack_f = jnp.pad(pack_f, ((0, 0), (0, -used_f % unit), (0, 0)))
-    dkv = jnp.concatenate([grad_key_seqs, grad_value_seqs], axis=-1).astype(bf16)
-    dkv = jnp.swapaxes(
-        dkv.reshape(seq_count, ctx_count, pair_rows, 2 * k_width), 0, 1
-    ).reshape(ctx_count, row_count, 2 * k_width)
+        [query_rows, all_kv, bias, mixed_rows, grad_mixed, log_sums],
+        3 * flops,
+    )
     own_kv, part_f = kv_back(ctx_count, dkv, pack_f, 2)
     own_key_grad, own_value_grad = own_kv[:, :k_width], own_kv[:, k_width:]
     grad_query_lin = (
-        rotate(grad_query_seqs.reshape(row_count, HQ, HD), cosine, -sine)
+        rotate(grad_query_rows.reshape(row_count, HQ, HD), cosine, -sine)
         .reshape(row_count, HQ * HD)
         .astype(bf16)
     )

time: 460 us -> 298 us (0.65); the launches traced: 451 us -> 294 us
  local copies, waits for them, and re-layouts: 151 us -> 41.6 us
  matrix products: 101 us -> 26.1 us
  Pallas kernels: 156 us -> 205 us
  other arithmetic: 40.3 us -> 18.3 us
    dot_general x45 -> x0, matrix products: 80 us -> none  [the longest x6 21.2 us: forward_group(): jnp.einsum('rqk,kd->qrd', probs, value_grp, preferred_element_type=f32)]
    pallas_call x0 -> x3, Pallas kernels: none -> 49.2 us  [plain_call(): pl.pallas_call(kernel, out_shape=out_shape, in_specs=[vm] * len(args), ou...]
    dynamic_update_slice x10 -> x0, local copies, waits for them, and re-layouts: 39 us -> none  [the longest x6 34.4 us: shards(): lax.map(backward_seq, (query_seqs, all_keys, all_values, grad_mixed_seqs,...]
    reshape x11 -> x0, local copies, waits for them, and re-layouts: 38.6 us -> none  [the longest x2 12 us: shards(): dw_gu.reshape(4, piece, 4, slab)]
    concatenate x4 -> x0, local copies, waits for them, and re-layouts: 8.73 us -> none  [the longest x2 8.58 us: shards(): jnp.concatenate([grad_key_seqs, grad_value_seqs], axis=-1).astype(bf16)]
    reduce_sum x6 -> x0, other arithmetic: 8.37 us -> none  [forward_group(): row_sum = jnp.sum(raised, axis=-1, keepdims=True)]
    while x60 -> x0, local copies, waits for them, and re-layouts: 7.97 us -> none
    transpose x7 -> x2, local copies, waits for them, and re-layouts: 8.77 us -> 2.11 us  [shards(): pack_f = plain_call(pack_kernel, jax.ShapeDtypeStruct((4, rows_f, slab),...]
where the time goes in v2:
time: 298 us; the launch traced here: 294 us
  Pallas kernels  205 us (69%)
  local copies, waits for them, and re-layouts  41.6 us (14%)
  matrix products  26.1 us (9%)
  other arithmetic  18.3 us (6%)
    pallas_call x4, Pallas kernels, comm_call(): pl.pallas_call(kernel, out_shape=out_shape, in_specs=[vm] * len(args), ou...  156 us
    pallas_call x3, Pallas kernels, plain_call(): pl.pallas_call(kernel, out_shape=out_shape, in_specs=[vm] * len(args), ou...  49.2 us
    unnamed x58, local copies, waits for them, and re-layouts  11.2 us
    dot_general x1, matrix products, shards(): gate_up = jnp.dot(second_in, gu_all, preferred_element_type=f32)  7.07 us
    dot_general x1, matrix products, shards(): jnp.einsum('rd,fd->rf', grad_branch, wd_all, preferred_element_type=f32)  6.14 us

profile of v2, /device:TPU:0, one launch (start us, length us, event | category | flops | bytes accessed | tf_op | source)
XLA Modules:
  0.0 293.9 jit_solution(8745463873627260021)
XLA Ops:
  0.7 1.9 pad_maximum_fusion.8.refs_0_
  4.6 14.0 %shard_map.212 = (bf16[576,960]{1,0:T(8,128)(2,1)}, bf16[64,144]{1,0:T(8,128)(2,1)}) custom-call(bf16[144,960]{1,0:T(8,128)(2,1)} %pad_maximum_fusion.8.refs_0_, bf16[16,144]{1,0:T(8,128)(2,1)} %maximum_maximum_fusion.refs_1_), custom_call_target="tpu_custom_call" | custom-call | tf_op jit(solution)/shard_map/pallas_call | solution.py:92
  25.4 1.9 pad_maximum_fusion.7.kv_ref
  27.4 2.1 pad_maximum_fusion.3.refs_1_
  29.5 2.0 copy.81.refs_2_
  31.5 43.9 %shard_map.213 = (bf16[8,512,384]{2,1,0:T(8,128)(2,1)}, bf16[576,576]{1,0:T(8,128)(2,1)}, bf16[576,3072]{1,0:T(8,128)(2,1)}, bf16[1536,576]{1,0:T(8,128)(2,1)}) custom-call(bf16[512,384]{1,0:T(8,128)(2,1)} %pad_maximum_fusion.7.kv_ref, bf16[144,576]{1,0:T(8,128)(2,1)} %refs_0_.1, bf16[144,3072]{1,0:T(8,128)(2,1)} %pad_maximum_fusion.3.refs_1_, ...), custom_call_target="tpu_custom_call" | custom-call | tf_op jit(solution)/shard_map/pallas_call | solution.py:92
  80.9 16.2 %shard_map.214 = (bf16[512,576]{1,0:T(8,128)(2,1)}, f32[512,128]{1,0:T(8,128)}) custom-call(bf16[512,576]{1,0:T(8,128)(2,1)} %copy.82.q_ref, bf16[8,512,384]{2,1,0:T(8,128)(2,1)} %get-tuple-element.27.kv_ref, f32[2,128,1024]{2,1,0:T(8,128)} %pad_maximum_fusion.1.bias_ref), custom_call_target="tpu_custom_call" | custom-call | flops 2415919104 | bytes 8000000 | tf_op jit(solution)/shard_map/pallas_call | solution.py:654
  97.1 1.9 multiply_reduce_fusion.2
  99.1 7.1 %fusion.18 = f32[512,3072]{1,0:T(8,128)} fusion(bf16[576,3072]{1,0:T(8,128)(2,1)} %get-tuple-element.30, f32[512,576]{1,0:T(8,128)S(1)} %get-tuple-element.104, f32[576]{0:T(1024)S(1)} %reshape.411, f32[512]{0:T(512)S(1)} %get-tuple-element.100), kind=kOutput, calls=%fused_computation.78 | convolution fusion | flops 1812824064 | bytes 11014400 | tf_op jit(solution)/shard_map/dot_general | solution.py:770
  107.6 6.1 %multiply_convert_fusion.1 = (bf16[512,1536]{1,0:T(8,128)(2,1)S(1)}, bf16[512,1536]{1,0:T(8,128)(2,1)S(1)}, bf16[512,1536]{1,0:T(8,128)(2,1)}) fusion(f32[512,3072]{1,0:T(8,128)} %fusion.18, bf16[1536,576]{1,0:T(8,128)(2,1)} %get-tuple-element.31, bf16[512,576]{1,0:T(8,128)(2,1)S(1)} %bitcast.88), kind=kOutput, calls=%fused_computation.3 | convolution fusion | flops 918552576 | bytes 13369344 | tf_op jit(solution)/shard_map/rd,fd->rf/dot_general | solution.py:778
  113.7 2.8 multiply_reduce_fusion
  116.5 1.8 fusion.20
  121.0 23.6 %shard_map.215 = (f32[512,576]{1,0:T(8,128)}, bf16[8,512,384]{2,1,0:T(8,128)(2,1)}) custom-call(bf16[512,576]{1,0:T(8,128)(2,1)} %copy.82.q_ref, bf16[8,512,384]{2,1,0:T(8,128)(2,1)} %get-tuple-element.27.kv_ref, f32[2,128,1024]{2,1,0:T(8,128)} %pad_maximum_fusion.1.bias_ref, bf16[512,576]{1,0:T(8,128)(2,1)} %get-tuple-element.28.o_ref, ...), custom_call_target="tpu_custom_call" | custom-call | flops 7247757312 | bytes 8000000 | tf_op jit(solution)/shard_map/pallas_call | solution.py:654
  144.6 1.7 copy.90
  147.9 3.4 %pad_maximum_fusion.gu_ref = bf16[512,3072]{1,0:T(8,128)(2,1)} fusion(bf16[512,1536]{1,0:T(8,128)(2,1)} %copy-done.11, bf16[512,1536]{1,0:T(8,128)(2,1)S(1)} %copy-done.10), kind=kLoop, calls=%fused_computation.1 | loop fusion | flops 6291456 | bytes 6291456 | tf_op jit(solution)/shard_map/concatenate | solution.py:784
  155.3 9.4 %shard_map.216.pack = bf16[4,1024,768]{2,1,0:T(8,128)(2,1)} custom-call(bf16[576,512]{1,0:T(8,128)(2,1)} %copy.94.second_t, bf16[512,3072]{1,0:T(8,128)(2,1)} %pad_maximum_fusion.gu_ref, bf16[576,512]{1,0:T(8,128)(2,1)} %copy.95.branch_t, bf16[512,1536]{1,0:T(8,128)(2,1)} %get-tuple-element.82.hidden_ref, bf16[576,512]{1,0:T(8,128)(2,1)} %bitcast.106, ...), custom_call_target="tpu_custom_call" | custom-call | flops 7247757312 | bytes 8000000 | tf_op jit(solution)/shard_map/pallas_call | solution.py:654
  164.7 45.7 %shard_map.217 = (f32[512,384]{1,0:T(8,128)}, bf16[1024,768]{1,0:T(8,128)(2,1)}) custom-call(bf16[8,512,384]{2,1,0:T(8,128)(2,1)} %get-tuple-element.34.dkv, bf16[4,1024,768]{2,1,0:T(8,128)(2,1)} %shard_map.216.pack), custom_call_target="tpu_custom_call" | custom-call | tf_op jit(solution)/shard_map/pallas_call | solution.py:92
  215.2 1.7 reshape.401
  216.9 1.5 copy.99
  218.6 2.2 fusion.9
  222.1 52.4 %shard_map.218 = (bf16[1024,768]{1,0:T(8,128)(2,1)}, bf16[640,256]{1,0:T(8,128)(2,1)}) custom-call(bf16[1024,768]{1,0:T(8,128)(2,1)} %get-tuple-element.36.part, bf16[4,640,256]{2,1,0:T(8,128)(2,1)} %pad.19.pack), custom_call_target="tpu_custom_call" | custom-call | tf_op jit(solution)/shard_map/pallas_call | solution.py:92
  279.0 2.6 reshape.407
  281.5 2.2 copy.104
  289.1 3.4 %fusion.1 = bf16[512,576]{1,0:T(8,128)(2,1)S(1)} fusion(f32[512,576]{1,0:T(8,128)S(1)} %copy-done.2, bf16[512,1536]{1,0:T(8,128)(2,1)} %get-tuple-element.82.hidden_ref, bf16[1536,576]{1,0:T(8,128)(2,1)} %get-tuple-element.31), kind=kOutput, calls=%fused_computation.11 | convolution fusion | flops 906559488 | bytes 5111808 | tf_op jit(solution)/shard_map/dot_general | solution.py:774
  (126 shorter events, 39.5 us)
Async XLA Ops:
  0.6 18.9 %copy-start.8 = (bf16[2,1,256,576]{2,3,1,0:T(8,128)(2,1)S(1)}, bf16[2,1,256,576]{2,3,1,0:T(8,128)(2,1)}, u32[]{:S(2)}) copy-start(bf16[2,1,256,576]{2,3,1,0:T(8,128)(2,1)} %param.13) | copy-start | bytes 1769476
  19.8 1.3 copy-start.13
  20.2 1.9 copy-start.5
  21.1 1.0 copy-start.23
  76.4 1.2 copy-start.25
  80.9 16.2 %copy-start.16 = (bf16[576,576]{1,0:T(8,128)(2,1)S(1)}, bf16[576,576]{1,0:T(8,128)(2,1)}, u32[]{:S(2)}) copy-start(bf16[576,576]{1,0:T(8,128)(2,1)} %get-tuple-element.29) | copy-start | bytes 1990660
  99.0 17.5 %copy-start.1 = (f32[512,576]{1,0:T(8,128)}, f32[512,576]{1,0:T(8,128)S(1)}, u32[]{:S(2)}) copy-start(f32[512,576]{1,0:T(8,128)S(1)} %get-tuple-element.104) | copy-start | bytes 3538948
  107.6 6.2 %copy-start.24 = (bf16[576,3072]{1,0:T(8,128)(2,1)S(1)}, bf16[576,3072]{1,0:T(8,128)(2,1)}, u32[]{:S(2)}) copy-start(bf16[576,3072]{1,0:T(8,128)(2,1)} %get-tuple-element.30) | copy-start | bytes 10616836
  113.7 2.8 copy-start.9
  113.7 2.8 copy-start.11
  116.5 2.7 copy-start.17
  118.4 0.9 copy-start.18
  144.6 1.7 copy-start.20
  146.3 1.6 copy-start.10
  147.9 3.4 %copy-start.7 = (bf16[576,512]{0,1:T(8,128)(2,1)S(1)}, bf16[576,512]{0,1:T(8,128)(2,1)}, u32[]{:S(2)}) copy-start(bf16[576,512]{0,1:T(8,128)(2,1)} %get-tuple-element.85) | copy-start | bytes 1769476
  151.4 1.8 copy-start.4
  211.5 2.6 copy-start.6
  211.5 2.6 copy-start.19
  216.9 1.6 copy-start.14
  276.0 2.1 copy-start
  281.5 2.2 copy-start.15
  283.8 3.5 %copy-start.12 = (f32[512,576]{1,0:T(8,128)S(1)}, f32[512,576]{1,0:T(8,128)}, u32[]{:S(2)}) copy-start(f32[512,576]{1,0:T(8,128)} %get-tuple-element.106) | copy-start | bytes 3538948
  283.8 3.5 %copy-start.3 = (f32[512,576]{1,0:T(8,128)S(1)}, f32[512,576]{1,0:T(8,128)}, u32[]{:S(2)}) copy-start(f32[512,576]{1,0:T(8,128)} %get-tuple-element.79) | copy-start | bytes 3538948
  287.7 1.4 copy-start.2
  (2 other events, 1.5 us)

commit v3 on v2

--- a/solution.py
+++ b/solution.py
@@ -125,10 +125,10 @@
         for _, _, _, src, dst, shard, rows in self.parts:
             dst[pl.ds(pl.multiple_of(shard * rows, 16), rows)] = src[...]
 
-    def forward(self):
-        for cross, _, onward, *_ in self.parts:
-            cross.wait_recv()
-            onward.start()
+    def forward(self, k):
+        cross, _, onward = self.parts[k][:3]
+        cross.wait_recv()
+        onward.start()
 
     def finish(self):
         for cross, near, onward, *_ in self.parts:
@@ -146,7 +146,8 @@
     greet((core, across))
     work = WeightGather(ins, outs, sems, 0, shard, core, across)
     work.start()
-    work.forward()
+    for j in range(k):
+        work.forward(j)
     work.finish()
 
 
@@ -170,34 +171,47 @@
     half = count // 2
     rows = kv_ref.shape[0]
 
-    def step(t, way):
+    def step(t, way, sub):
         block = ring_index(place - way * (t - 1), count)
         src = kv_ref if t == 1 else all_ref.at[block]
-        dst = all_ref.at[block]
-        if t == half:
-            cut = pl.ds(0, rows // 2) if way > 0 else pl.ds(rows // 2, rows // 2)
-            src, dst = src.at[cut], dst.at[cut]
+        cut = pl.ds(sub * (rows // 2), rows // 2)
         lane = 0 if way > 0 else 1
         return remote(
-            src, dst, ring.at[0, lane, t - 1], ring.at[1, lane, t - 1], right if way > 0 else left
+            src.at[cut],
+            all_ref.at[block, cut],
+            ring.at[0, lane, t - 1, sub],
+            ring.at[1, lane, t - 1, sub],
+            right if way > 0 else left,
         )
 
-    steps = [(step(t, 1), step(t, -1)) for t in range(1, half + 1)]
-    steps[0][0].start()
-    steps[0][1].start()
+    def group(t):
+        if t == half:
+            return [step(t, 1, 0), step(t, -1, 1)]
+        return [step(t, 1, 0), step(t, -1, 1), step(t, 1, 1), step(t, -1, 0)]
+
+    steps = [group(t) for t in range(1, half + 1)]
+    for copy in steps[0]:
+        copy.start()
     work = WeightGather(ins, outs, sems, 0, shard, core, across)
     work.start()
     all_ref[me] = kv_ref[...]
+    sent = 0
     for t in range(1, half):
-        for way in (0, 1):
-            steps[t - 1][way].wait_recv()
-            steps[t][way].start()
-    work.forward()
-    for way in (0, 1):
-        steps[half - 1][way].wait_recv()
+        if sent < k:
+            work.forward(sent)
+            sent += 1
+        for j, copy in enumerate(steps[t - 1]):
+            copy.wait_recv()
+            if j < len(steps[t]):
+                steps[t][j].start()
+    while sent < k:
+        work.forward(sent)
+        sent += 1
+    for copy in steps[half - 1]:
+        copy.wait_recv()
     for pair in steps:
-        pair[0].wait_send()
-        pair[1].wait_send()
+        for copy in pair:
+            copy.wait_send()
     work.finish()
 
 
@@ -209,14 +223,16 @@
         outs,
         [
             pltpu.SemaphoreType.DMA((2, len(arrays), 3)),
-            pltpu.SemaphoreType.DMA((2, 2, count // 2)),
+            pltpu.SemaphoreType.DMA((2, 2, count // 2, 2)),
         ],
         cid,
         [kv] + list(arrays),
     )
 
 
-def add_rows(rows, block, body):
+def add_rows(rows, width, body):
+    block = max(b for b in range(16, 129, 16) if rows % b == 0 and b * width <= 64 * 768)
+
     def one(i, carry):
         body(pl.ds(pl.multiple_of(i * block, 16), block))
         return carry
@@ -228,7 +244,7 @@
     def __init__(self, pack, out, near_buf, far_buf, sems, chunks, shard, core, across):
         self.pack, self.out, self.near_buf, self.far_buf = pack, out, near_buf, far_buf
         self.size = pack.shape[1] // chunks
-        self.chunks = chunks
+        self.chunks, self.width = chunks, pack.shape[2]
         self.mine, self.side = lax.rem(shard, 2), shard // 2
         self.near, self.far = [], []
         for c in range(chunks):
@@ -272,7 +288,7 @@
                 self.near_buf[x, cut] = total.astype(jnp.bfloat16)
 
         base = c * self.size
-        add_rows(self.size, 16, lambda cut: body(pl.ds(pl.multiple_of(base + cut.start, 16), cut.size)))
+        add_rows(self.size, self.width, lambda cut: body(pl.ds(pl.multiple_of(base + cut.start, 16), cut.size)))
         self.far[c].start()
 
     def close(self, c):
@@ -286,7 +302,7 @@
             self.out[cut] = total.astype(jnp.bfloat16)
 
         base = c * self.size
-        add_rows(self.size, 16, lambda cut: body(pl.ds(pl.multiple_of(base + cut.start, 16), cut.size)))
+        add_rows(self.size, self.width, lambda cut: body(pl.ds(pl.multiple_of(base + cut.start, 16), cut.size)))
 
     def finish(self):
         for pair in self.near:
@@ -298,7 +314,7 @@
     def __init__(self, count, term, rows, cuts, send_buf, recv_buf, sems, place, right, left):
         self.count, self.term, self.rows, self.cuts = count, term, rows, cuts
         self.send_buf, self.recv_buf, self.place = send_buf, recv_buf, place
-        self.half = count // 2
+        self.half, self.width = count // 2, send_buf.shape[3]
         self.copies = []
         for t in range(self.half):
             pair = []
@@ -344,7 +360,7 @@
                     )
                     self.send_buf[lane, t, cut] = total.astype(jnp.bfloat16)
 
-                add_rows(self.rows, 16, body)
+                add_rows(self.rows, self.width, body)
             self.copies[t][lane].start()
 
     def last(self, store):
@@ -360,7 +376,7 @@
             )
             store(cut, total)
 
-        add_rows(self.rows, 16, body)
+        add_rows(self.rows, self.width, body)
 
     def finish(self):
         for pair in self.copies:
@@ -380,15 +396,20 @@
     turn.start()
     shares = ShardSum(pack, sum_ref, near_buf, far_buf, sems, chunks, shard, core, across)
     shares.start()
-    for c in range(chunks):
-        shares.cross(c)
+    shares.cross(0)
     for t in range(1, half):
+        if t == half - 1:
+            for c in range(chunks // 2):
+                shares.close(c)
         turn.step(t)
+        if t == 1:
+            for c in range(1, chunks):
+                shares.cross(c)
 
     def store(cut, total):
         own_ref[cut] = total
 
-    for c in range(chunks):
+    for c in range(chunks // 2, chunks):
         shares.close(c)
     turn.last(store)
     turn.finish()
@@ -661,7 +682,7 @@
     )(*args)
 
 
-def pack_kernel(second_t, gu_ref, branch_t, hidden_ref, mixed_t, ga_ref, gain_ref, out_ref):
+def pack_kernel(second_t, gate_ref, up_ref, branch_t, hidden_ref, mixed_t, ga_ref, gain_ref, out_ref):
     f32 = jnp.float32
     bf16 = jnp.bfloat16
     width = second_t.shape[0]
@@ -674,7 +695,9 @@
         mine = pl.ds(f * piece, piece)
         for s in range(4):
             out_ref[f, s * piece : (s + 1) * piece] = jnp.dot(
-                second_t[mine], gu_ref[:, s * slab : (s + 1) * slab], preferred_element_type=f32
+                second_t[mine],
+                (gate_ref, up_ref)[s // 2][:, (s % 2) * slab : (s % 2 + 1) * slab],
+                preferred_element_type=f32,
             ).astype(bf16)
         for h in range(2):
             out_ref[f, 4 * piece : at, h * cols : (h + 1) * cols] = jnp.dot(
@@ -687,6 +710,35 @@
         ).astype(bf16)
         out_ref[f, at : at + piece, width:] = jnp.zeros((piece, slab - width), bf16)
         out_ref[f, at + piece :] = gain_ref[f]
+
+
+def unpack_kernel(f_ref, q_ref, *outs):
+    f32 = jnp.float32
+    query, key, value, out, gate, up, down, gain_one, gain_two = outs
+    piece, width = query.shape
+    slab, narrow = f_ref.shape[1], q_ref.shape[1]
+    cols, deep = down.shape[0], width // 2
+    for s in range(4):
+        (gate, up)[s // 2][:, (s % 2) * slab : (s % 2 + 1) * slab] = f_ref[
+            s * piece : (s + 1) * piece
+        ].astype(f32)
+    at = 4 * piece
+    for h in range(2):
+        block = f_ref[at : at + deep, h * cols : (h + 1) * cols].astype(f32)
+        down[:, h * deep : (h + 1) * deep] = block.T
+    at += deep
+    out[...] = f_ref[at : at + piece, :width].astype(f32)
+    gain_two[...] = f_ref[at + piece : at + piece + 16, :piece].astype(f32)[:1]
+    total = width + 2 * key.shape[1]
+    strips = -(-total // narrow)
+    wide = jnp.concatenate(
+        [q_ref[s * piece : (s + 1) * piece].astype(f32) for s in range(strips)], axis=1
+    )
+    query[...] = wide[:, :width]
+    key[...] = wide[:, width : width + key.shape[1]]
+    value[...] = wide[:, width + key.shape[1] : total]
+    at = strips * piece
+    gain_one[...] = q_ref[at : at + 16, :piece].astype(f32)[:1]
 
 
 def shards(
@@ -747,10 +799,10 @@
         qkv_rows[:, q_width : q_width + k_width].reshape(row_count, HK, HD), cosine, sine
     ).astype(bf16)
     value_rows = qkv_rows[:, q_width + k_width :].astype(bf16)
-    all_kv, wo_all, gu_all, wd_all = gather_both(
+    all_kv, wo_all, wg_all, wu_all, wd_all = gather_both(
         ctx_count,
         jnp.concatenate([key_rows.reshape(row_count, k_width), value_rows], axis=1),
-        [w_out, jnp.concatenate([w_gate, w_up], axis=1), w_down],
+        [w_out, w_gate, w_up, w_down],
         1,
     )
     query_rows = query_rows.reshape(row_count, q_width) * jnp.asarray(score_scale, bf16)
@@ -767,9 +819,9 @@
     middle = x_rows + jnp.dot(mixed_rows, wo_all, preferred_element_type=f32)
     inverse_two = lax.rsqrt(jnp.mean(middle * middle, axis=-1, keepdims=True) + EPS)
     second_in = (middle * inverse_two * gain_second.astype(f32)).astype(bf16)
-    gate_up = jnp.dot(second_in, gu_all, preferred_element_type=f32)
-    hidden_width = gate_up.shape[1] // 2
-    gate_proj, up_proj = gate_up[:, :hidden_width], gate_up[:, hidden_width:]
+    gate_proj = jnp.dot(second_in, wg_all, preferred_element_type=f32)
+    up_proj = jnp.dot(second_in, wu_all, preferred_element_type=f32)
+    hidden_width = gate_proj.shape[1]
     hidden = (jax.nn.silu(gate_proj) * up_proj).astype(bf16)
     out_rows = middle + jnp.dot(hidden, wd_all, preferred_element_type=f32)
     result = out_rows.astype(bf16).reshape(hidden_in.shape)
@@ -781,8 +833,9 @@
         grad_hidden * up_proj * sigmoid_gate * (1.0 + gate_proj * (1.0 - sigmoid_gate))
     ).astype(bf16)
     grad_up_proj = (grad_hidden * gate_proj * sigmoid_gate).astype(bf16)
-    grad_gu = jnp.concatenate([grad_gate_proj, grad_up_proj], axis=1)
-    grad_second = jnp.einsum("rf,df->rd", grad_gu, gu_all, preferred_element_type=f32)
+    grad_second = jnp.einsum(
+        "rf,df->rd", grad_gate_proj, wg_all, preferred_element_type=f32
+    ) + jnp.einsum("rf,df->rd", grad_up_proj, wu_all, preferred_element_type=f32)
     grad_norm_two, dg_second = norm_back(
         middle, inverse_two, gain_second.astype(f32), grad_second
     )
@@ -792,8 +845,7 @@
         bf16
     )
     piece = width // 4
-    slab = grad_gu.shape[1] // 4
-    down_cols = hidden_width // 4
+    slab = hidden_width // 2
     unit = 16 * ctx_count
     used_f = 5 * piece + width // 2
     rows_f = -(-(used_f + 1) // unit) * unit
@@ -804,7 +856,7 @@
     pack_f = plain_call(
         pack_kernel,
         jax.ShapeDtypeStruct((4, rows_f, slab), bf16),
-        [second_in.T, grad_gu, grad_branch.T, hidden, mixed_rows.T, grad_attn, gain_rows],
+        [second_in.T, grad_gate_proj, grad_up_proj, grad_branch.T, hidden, mixed_rows.T, grad_attn, gain_rows],
         3 * flops,
     )
     grad_query_rows, dkv = plain_call(
@@ -849,28 +901,29 @@
     )
     pack_q = jnp.pad(pack_q, ((0, 0), (0, -pack_q.shape[1] % unit), (0, 0)))
     total_f, total_q = last_sum(ctx_count, part_f, pack_q, 3)
-    total_f, total_q = total_f.astype(f32), total_q.astype(f32)
-    out_gu = jnp.swapaxes(total_f[: 4 * piece].reshape(4, piece, slab), 0, 1).reshape(piece, -1)
-    at = 4 * piece
-    out_down = total_f[at : at + width // 2].reshape(width // 2, 2, down_cols)
-    out_down = jnp.swapaxes(out_down, 0, 1).reshape(width, down_cols).T
-    at += width // 2
-    out_wo = total_f[at : at + piece, :width]
-    out_g2 = total_f[at + piece, :piece]
-    at = strips * piece
-    out_qkv = jnp.swapaxes(total_q[:at].reshape(strips, piece, narrow), 0, 1).reshape(piece, -1)
+    shapes = [
+        (piece, q_width),
+        (piece, k_width),
+        (piece, k_width),
+        w_out.shape,
+        w_gate.shape,
+        w_up.shape,
+        w_down.shape,
+        (1, piece),
+        (1, piece),
+    ]
+    grads = plain_call(
+        unpack_kernel,
+        [jax.ShapeDtypeStruct(shape, f32) for shape in shapes],
+        [total_f, total_q],
+        1_000_000,
+    )
     return (
         result,
         grad_in_rows.reshape(hidden_in.shape),
-        out_qkv[:, :q_width],
-        out_qkv[:, q_width : q_width + k_width],
-        out_qkv[:, q_width + k_width : q_width + 2 * k_width],
-        out_wo,
-        out_gu[:, :hidden_width],
-        out_gu[:, hidden_width:],
-        out_down,
-        total_q[at, :piece],
-        out_g2,
+        *grads[:7],
+        grads[7].reshape(piece),
+        grads[8].reshape(piece),
     )
 
 

time: 298 us -> 309 us (1.037)
  matrix products: 26.1 us -> 29.3 us
    slice x9 -> x0, local copies, waits for them, and re-layouts: 7.06 us -> none  [the longest x1 1.33 us: shards(): out_gu[:, hidden_width:]]
    concatenate x2 -> x0, other arithmetic: 5.57 us -> none  [the longest x1 3.44 us: shards(): grad_gu = jnp.concatenate([grad_gate_proj, grad_up_proj], axis=1)]
    unnamed x58 -> x49, local copies, waits for them, and re-layouts: 11.2 us -> 14.7 us
    slice x4, local copies, waits for them, and re-layouts: 2.56 us -> 5.89 us  [shards(): own_key_grad, own_value_grad = (own_kv[:, :k_width], own_kv[:, k_width:])]
    pallas_call x3 -> x4, Pallas kernels: 49.2 us -> 52.4 us  [plain_call(): pl.pallas_call(kernel, out_shape=out_shape, in_specs=[vm] * len(args), ou...]
    dot_general x2 -> x4, matrix products: 9.83 us -> 10.9 us  [the longest x1 4.75 us: shards(): up_proj = jnp.dot(second_in, wu_all, preferred_element_type=f32)]
where the time goes in v3:
time: 309 us; the launch traced here: 304 us
  Pallas kernels  208 us (67%)
  local copies, waits for them, and re-layouts  44.4 us (14%)
  matrix products  29.3 us (9%)
  other arithmetic  19.5 us (6%)
    pallas_call x4, Pallas kernels, comm_call(): pl.pallas_call(kernel, out_shape=out_shape, in_specs=[vm] * len(args), ou...  156 us
    pallas_call x4, Pallas kernels, plain_call(): pl.pallas_call(kernel, out_shape=out_shape, in_specs=[vm] * len(args), ou...  52.4 us
    unnamed x49, local copies, waits for them, and re-layouts  14.7 us

profile of v3, /device:TPU:0, one launch (start us, length us, event | category | flops | bytes accessed | tf_op | source)
XLA Modules:
  0.0 304.0 jit_solution(2632928999556712912)
XLA Ops:
  4.6 14.1 %shard_map.212 = (bf16[576,960]{1,0:T(8,128)(2,1)}, bf16[64,144]{1,0:T(8,128)(2,1)}) custom-call(bf16[144,960]{1,0:T(8,128)(2,1)} %pad_maximum_fusion.6.refs_0_, bf16[16,144]{1,0:T(8,128)(2,1)} %maximum_maximum_fusion.refs_1_), custom_call_target="tpu_custom_call" | custom-call | tf_op jit(solution)/shard_map/pallas_call | solution.py:92
  29.4 44.2 %shard_map.213 = (bf16[8,512,384]{2,1,0:T(8,128)(2,1)}, bf16[576,576]{1,0:T(8,128)(2,1)}, bf16[576,1536]{1,0:T(8,128)(2,1)}, bf16[576,1536]{1,0:T(8,128)(2,1)}, bf16[1536,576]{1,0:T(8,128)(2,1)}) custom-call(bf16[512,384]{1,0:T(8,128)(2,1)} %pad_maximum_fusion.5.kv_ref, bf16[144,576]{1,0:T(8,128)(2,1)} %refs_0_.1, bf16[144,1536]{1,0:T(8,128)(2,1)} %refs_1_.1, ...), custom_call_target="tpu_custom_call" | custom-call | tf_op jit(solution)/shard_map/pallas_call | solution.py:92
  79.1 15.8 %shard_map.214 = (bf16[512,576]{1,0:T(8,128)(2,1)}, f32[512,128]{1,0:T(8,128)}) custom-call(bf16[512,576]{1,0:T(8,128)(2,1)} %copy.78.q_ref, bf16[8,512,384]{2,1,0:T(8,128)(2,1)} %get-tuple-element.37.kv_ref, f32[2,128,1024]{2,1,0:T(8,128)} %pad_maximum_fusion.bias_ref), custom_call_target="tpu_custom_call" | custom-call | flops 2415919104 | bytes 8000000 | tf_op jit(solution)/shard_map/pallas_call | solution.py:675
  97.0 4.7 %fusion.20 = f32[512,1536]{1,0:T(8,128)} fusion(bf16[576,1536]{1,0:T(8,128)(2,1)} %get-tuple-element.41, f32[512,576]{1,0:T(8,128)S(1)} %get-tuple-element.119, f32[576]{0:T(1024)S(1)} %reshape.395, f32[512]{0:T(512)S(1)} %get-tuple-element.115), kind=kOutput, calls=%fused_computation.79 | convolution fusion | flops 906854400 | bytes 6099200 | tf_op jit(solution)/shard_map/dot_general | solution.py:823
  101.7 3.1 %fusion.19 = f32[512,1536]{1,0:T(8,128)} fusion(bf16[576,1536]{1,0:T(8,128)(2,1)S(1)} %copy-done.4, f32[512,576]{1,0:T(8,128)S(1)} %get-tuple-element.119, f32[576]{0:T(1024)S(1)} %reshape.395, f32[512]{0:T(512)S(1)} %get-tuple-element.115), kind=kOutput, calls=%fused_computation.78 | convolution fusion | flops 906854400 | bytes 6099200 | tf_op jit(solution)/shard_map/dot_general | solution.py:822
  106.2 6.2 %multiply_convert_fusion = (bf16[512,1536]{1,0:T(8,128)(2,1)S(1)}, bf16[512,1536]{1,0:T(8,128)(2,1)S(1)}, bf16[512,1536]{1,0:T(8,128)(2,1)}) fusion(f32[512,1536]{1,0:T(8,128)} %fusion.19, f32[512,1536]{1,0:T(8,128)} %fusion.20, bf16[1536,576]{1,0:T(8,128)(2,1)} %get-tuple-element.42, bf16[512,576]{1,0:T(8,128)(2,1)S(1)} %bitcast.78), kind=kOutput, calls=%fused_computation.1 | convolution fusion | flops 918552576 | bytes 13369344 | tf_op jit(solution)/shard_map/rd,fd->rf/dot_general | solution.py:830
  120.5 2.1 copy.86.do_ref
  122.6 23.6 %shard_map.215 = (f32[512,576]{1,0:T(8,128)}, bf16[8,512,384]{2,1,0:T(8,128)(2,1)}) custom-call(bf16[512,576]{1,0:T(8,128)(2,1)} %copy.78.q_ref, bf16[8,512,384]{2,1,0:T(8,128)(2,1)} %get-tuple-element.37.kv_ref, f32[2,128,1024]{2,1,0:T(8,128)} %pad_maximum_fusion.bias_ref, bf16[512,576]{1,0:T(8,128)(2,1)} %get-tuple-element.38.o_ref, ...), custom_call_target="tpu_custom_call" | custom-call | flops 7247757312 | bytes 8000000 | tf_op jit(solution)/shard_map/pallas_call | solution.py:675
  146.2 2.7 copy.87
  152.3 2.1 copy.90.second_t
  155.2 2.1 copy.88
  158.3 9.4 %shard_map.216.pack = bf16[4,1024,768]{2,1,0:T(8,128)(2,1)} custom-call(bf16[576,512]{1,0:T(8,128)(2,1)} %copy.90.second_t, bf16[512,1536]{1,0:T(8,128)(2,1)} %copy-done.20, bf16[512,1536]{1,0:T(8,128)(2,1)} %copy-done.19, bf16[576,512]{1,0:T(8,128)(2,1)} %copy.91.branch_t, bf16[512,1536]{1,0:T(8,128)(2,1)} %get-tuple-element.102.hidden_ref, ...), custom_call_target="tpu_custom_call" | custom-call | flops 7247757312 | bytes 8000000 | tf_op jit(solution)/shard_map/pallas_call | solution.py:675
  167.7 45.5 %shard_map.217 = (f32[512,384]{1,0:T(8,128)}, bf16[1024,768]{1,0:T(8,128)(2,1)}) custom-call(bf16[8,512,384]{2,1,0:T(8,128)(2,1)} %get-tuple-element.45.dkv, bf16[4,1024,768]{2,1,0:T(8,128)(2,1)} %shard_map.216.pack), custom_call_target="tpu_custom_call" | custom-call | tf_op jit(solution)/shard_map/pallas_call | solution.py:92
  215.1 2.0 copy.92
  220.9 2.2 convolution_convert_fusion
  224.3 3.5 %reshape.389 = bf16[4,144,4,256]{3,2,1,0:T(4,128)(2,1)} reshape(bf16[576,1024]{1,0:T(8,128)(2,1)} %pad.17) | data formatting | bytes 2359296 | tf_op jit(solution)/shard_map/reshape | solution.py:892
  227.8 2.6 copy.95
  230.5 2.2 fusion.9
  235.3 51.7 %shard_map.218 = (bf16[1024,768]{1,0:T(8,128)(2,1)}, bf16[640,256]{1,0:T(8,128)(2,1)}) custom-call(bf16[1024,768]{1,0:T(8,128)(2,1)} %get-tuple-element.47.part, bf16[4,640,256]{2,1,0:T(8,128)(2,1)} %pad.19.pack), custom_call_target="tpu_custom_call" | custom-call | tf_op jit(solution)/shard_map/pallas_call | solution.py:92
  287.0 3.6 %shard_map.219 = (f32[144,576]{1,0:T(8,128)}, f32[144,192]{1,0:T(8,128)}, f32[144,192]{1,0:T(8,128)}, f32[144,576]{1,0:T(8,128)}, f32[144,1536]{1,0:T(8,128)}, /...) custom-call(bf16[1024,768]{1,0:T(8,128)(2,1)} %get-tuple-element.48.f_ref, ...), custom_call_target="tpu_custom_call" | custom-call | flops 1000000 | bytes 8000000 | tf_op jit(solution)/shard_map/pallas_call | solution.py:675
  290.7 2.4 copy.100
  293.1 3.2 %fusion.6 = f32[512,576]{1,0:T(8,128)} fusion(f32[512,576]{1,0:T(8,128)} %get-tuple-element.99, f32[2,1,256,576]{3,2,0,1:T(8,128)S(1)} %copy.74, f32[512,576]{1,0:T(8,128)} %get-tuple-element.121, f32[512]{0:T(512)S(1)} %broadcast_multiply_fusion, f32[512]{0:T(512)S(1)} %multiply_multiply_fusion, f32[576]{0:T(1024)S(1)} %reshape.394, f32[512]{0:T(512)S(1)} %bitcast.97), kind=kLoop, calls=%fused_computation.21 | loop fusion | flops 1769472 | bytes 4727040 | tf_op jit(solution)/shard_map/add | solution.py:888
  296.3 2.7 copy.99
  299.0 3.4 %fusion.1 = bf16[512,576]{1,0:T(8,128)(2,1)S(1)} fusion(f32[512,576]{1,0:T(8,128)S(1)} %get-tuple-element.119, bf16[512,1536]{1,0:T(8,128)(2,1)} %get-tuple-element.102.hidden_ref, bf16[1536,576]{1,0:T(8,128)(2,1)} %get-tuple-element.42), kind=kOutput, calls=%fused_computation.11 | convolution fusion | flops 906559488 | bytes 5111808 | tf_op jit(solution)/shard_map/dot_general | solution.py:826
  (106 shorter events, 45.7 us)
Async XLA Ops:
  0.6 19.0 %copy-start.2 = (bf16[2,1,256,576]{2,3,1,0:T(8,128)(2,1)S(1)}, bf16[2,1,256,576]{2,3,1,0:T(8,128)(2,1)}, u32[]{:S(2)}) copy-start(bf16[2,1,256,576]{2,3,1,0:T(8,128)(2,1)} %param.13) | copy-start | bytes 1769476
  19.8 1.3 copy-start.6
  20.2 1.9 copy-start
  21.1 1.0 copy-start.17
  23.1 0.6 copy-start.13
  73.6 0.8 copy-start.14
  74.6 1.2 copy-start.18
  79.1 15.8 %copy-start.8 = (bf16[576,576]{1,0:T(8,128)(2,1)S(1)}, bf16[576,576]{1,0:T(8,128)(2,1)}, u32[]{:S(2)}) copy-start(bf16[576,576]{1,0:T(8,128)(2,1)} %get-tuple-element.39) | copy-start | bytes 1990660
  97.0 4.8 %copy-start.4 = (bf16[576,1536]{1,0:T(8,128)(2,1)S(1)}, bf16[576,1536]{1,0:T(8,128)(2,1)}, u32[]{:S(2)}) copy-start(bf16[576,1536]{1,0:T(8,128)(2,1)} %get-tuple-element.40) | copy-start | bytes 5308420
  106.2 6.2 %copy-start.5 = (bf16[576,1536]{1,0:T(8,128)(2,1)S(1)}, bf16[576,1536]{1,0:T(8,128)(2,1)}, u32[]{:S(2)}) copy-start(bf16[576,1536]{1,0:T(8,128)(2,1)} %get-tuple-element.40) | copy-start | bytes 5308420
  112.4 1.5 copy-start.20
  112.4 1.6 copy-start.19
  112.4 2.6 copy-start.3
  116.6 2.4 copy-start.9
  118.2 0.8 copy-start.10
  146.2 2.8 copy-start.12
  215.1 5.8 %copy-start.1 = (bf16[512,576]{1,0:T(8,128)(2,1)S(1)}, bf16[512,576]{1,0:T(8,128)(2,1)}, u32[]{:S(2)}) copy-start(bf16[512,576]{1,0:T(8,128)(2,1)} %copy-done) | copy-start | bytes 1769476
  227.8 2.6 copy-start.7
  227.8 2.6 copy-start.11
  227.8 2.6 copy-start.15
  227.8 2.6 copy-start.16
